TPU v7x, 128 devices: a whole 4x4x4 slice. The times are simulated.
128 devices in a mesh: req: 2 (over core), vocab: 64 (over x, y, z).
Axes of the slice: x: 4, y: 4, z: 4, core: 2. Of those that a mesh axis runs over, the one named last changes fastest.
Arguments:
- hidden: bfloat16 [512, 7168], P('req', 'vocab'), may hold values from -6000 to 6000
- next_embedding: bfloat16 [512, 7168], P('req', 'vocab'), may hold values from -6000 to 6000
- final_gain: bfloat16 [7168], P('vocab'), may hold values from 0.5 to 1.5
- hidden_gain: bfloat16 [7168], P('vocab'), may hold values from 0.5 to 1.5
- embed_gain: bfloat16 [7168], P('vocab'), may hold values from 0.5 to 1.5
- draft_gain: bfloat16 [7168], P('vocab'), may hold values from 0.5 to 1.5
- head_weight: bfloat16 [7168, 65536], P(None, 'vocab'), may hold values from -3 to 40
- proj_embed: bfloat16 [7168, 7168], P('vocab'), may hold values from -1 to 4
- proj_hidden: bfloat16 [7168, 7168], P('vocab'), may hold values from -0.1875 to 0.1875
- token_ids: int32 [512], P('req'), may hold values from 0 to 65535
- row_request: int32 [512], P('req'), may hold values from 0 to 63
Outputs:
- main_logprobs: float32 [512, 65536], P('req', 'vocab')
- draft_logprobs: float32 [512, 65536], P('req', 'vocab')
- request_score: float32 [64], replicated
All inputs are finite; a program needn't handle non-finite values.
Results may differ from a plain program's by a relative error of at most 0.0036.
Values may be sent and summed in bfloat16 or wider, within the bound.
A program may use at most 128 MiB of HBM per device.

v0:
```python
import jax
import jax.numpy as jnp
from jax import lax
from jax.sharding import PartitionSpec as P

D = 7168
REQS = 64


epsilon = 1e-06


def per_device(
    hidden,
    next_embedding,
    final_gain,
    hidden_gain,
    embed_gain,
    draft_gain,
    head_weight,
    proj_embed,
    proj_hidden,
    token_ids,
    row_request,
):
    vocab_local = head_weight.shape[1]
    contract_first = (((0,), (0,)), ((), ()))
    contract_cross = (((0,), (1,)), ((), ()))
    hidden_wide = hidden.astype(jnp.float32)
    embed_wide = next_embedding.astype(jnp.float32)
    hidden_sq, embed_sq = lax.psum(
        (jnp.sum(hidden_wide * hidden_wide, axis=1), jnp.sum(embed_wide * embed_wide, axis=1)),
        "vocab",
    )
    hidden_scale = lax.rsqrt(hidden_sq / D + epsilon)[:, None]
    embed_scale = lax.rsqrt(embed_sq / D + epsilon)[:, None]
    normed_final = (hidden_wide * hidden_scale * final_gain.astype(jnp.float32)[None, :]).astype(
        jnp.bfloat16
    )
    normed_hidden = (hidden_wide * hidden_scale * hidden_gain.astype(jnp.float32)[None, :]).astype(
        jnp.bfloat16
    )
    normed_embed = (embed_wide * embed_scale * embed_gain.astype(jnp.float32)[None, :]).astype(
        jnp.bfloat16
    )
    head_rows = head_weight
    main_logits = jnp.dot(
        lax.all_gather(normed_final, "vocab", axis=1, tiled=True),
        head_rows,
        preferred_element_type=jnp.float32,
    )
    draft_state = lax.psum_scatter(
        lax.dot_general(
            proj_embed, normed_embed, contract_cross, preferred_element_type=jnp.float32
        )
        + lax.dot_general(
            proj_hidden, normed_hidden, contract_cross, preferred_element_type=jnp.float32
        ),
        "vocab",
        scatter_dimension=0,
        tiled=True,
    )
    draft_sq = lax.psum(jnp.sum(draft_state * draft_state, axis=0), "vocab")
    normed_draft = (
        draft_state
        * lax.rsqrt(draft_sq / D + epsilon)[None, :]
        * draft_gain.astype(jnp.float32)[:, None]
    ).astype(jnp.bfloat16)
    head_rows = head_weight
    draft_logits = lax.dot_general(
        lax.all_gather(normed_draft, "vocab", axis=0, tiled=True),
        head_rows,
        contract_first,
        preferred_element_type=jnp.float32,
    )
    main_local = jnp.max(main_logits, axis=1)
    draft_local = jnp.max(draft_logits, axis=1)
    main_peak = lax.pmax(main_local, "vocab")
    main_sum = lax.psum(jnp.sum(jnp.exp(main_logits - main_peak[:, None]), axis=1), "vocab")
    main_logprobs = main_logits - (main_peak + jnp.log(main_sum))[:, None]
    draft_peak = lax.pmax(draft_local, "vocab")
    draft_sum = lax.psum(jnp.sum(jnp.exp(draft_logits - draft_peak[:, None]), axis=1), "vocab")
    draft_logprobs = draft_logits - (draft_peak + jnp.log(draft_sum))[:, None]
    columns = lax.axis_index("vocab") * vocab_local + lax.iota(jnp.int32, vocab_local)
    picked = jnp.sum(jnp.where(columns[None, :] == token_ids[:, None], main_logprobs, 0.0), axis=1)
    members = (row_request[:, None] == lax.iota(jnp.int32, REQS)[None, :]).astype(jnp.float32)
    partial_score = jnp.dot(picked, members, precision=lax.Precision.HIGHEST)
    request_score = lax.psum(partial_score, ("req", "vocab"))
    return (main_logprobs, draft_logprobs, request_score)


def solution(mesh):
    return jax.shard_map(
        per_device,
        mesh=mesh,
        in_specs=(
            P("req", "vocab"),
            P("req", "vocab"),
            P("vocab"),
            P("vocab"),
            P("vocab"),
            P("vocab"),
            P(None, "vocab"),
            P("vocab", None),
            P("vocab", None),
            P("req"),
            P("req"),
        ),
        out_specs=(P("req", "vocab"), P("req", "vocab"), P()),
        check_vma=False,
    )
```

profile of v0, /device:TPU:0, one launch (start us, length us, event | category | flops | bytes accessed | tf_op | source)
XLA Modules:
  0.0 1233.6 jit_solution(15311273476856027029)
XLA Ops:
  7.2 0.0 copy-start
  7.2 0.0 reduce-scatter.4.cloned.1.call-start
  7.2 1.0 fusion.5
  8.2 180.5 %all-reduce.1 = (f32[256]{0:T(256)S(1)}, f32[256]{0:T(256)S(1)}) all-reduce(f32[256]{0:T(256)S(1)} %get-tuple-element.15, f32[256]{0:T(256)S(1)} %get-tuple-element.16), channel_id=1, replica_groups=mesh['req'=2,'vocab'=64] {'vocab'}, use_global_device_ids=true, to_apply=%region_1.0 | all-reduce | flops 512 | bytes 4096 | tf_op jit(solution)/shard_map/psum | solution.py:31
  188.7 0.7 convert_element_type.35
  189.4 0.7 convert_element_type.37
  190.1 0.0 copy-done
  190.1 0.0 copy-start.1
  190.1 0.0 copy-start.2
  190.1 2.2 fusion.10
  192.2 0.0 copy-done.1
  192.2 0.0 copy-done.2
  192.2 4.2 fusion
  196.5 8.4 copy.16
  204.9 0.0 copy-start.5
  204.9 0.0 copy-start.6
  204.9 0.0 reduce-scatter.4.cloned.1.call-update
  204.9 0.0 all-gather.3.cloned.1.call-start
  204.9 0.6 copy-done.5
  205.5 0.7 fusion.3
  206.2 0.0 all-gather.3.cloned.1.call-update
  206.3 0.0 all-gather.5.cloned.1.call-start
  206.3 0.0 copy-done.6
  206.3 357.0 %reduce-scatter.4.cloned.1.call-done = f32[112,256]{1,0:T(8,128)} async-done(((f32[7168,256]{1,0:T(8,128)}), f32[112,256]{1,0:T(8,128)}) %reduce-scatter.4.cloned.1.call-update) | async-done | bytes 114704 | tf_op jit(solution)/shard_map/reduce_scatter | solution.py:52
  563.4 1.0 copy.17
  564.3 0.1 multiply_reduce_fusion
  564.5 172.6 %psum.45 = f32[256]{0:T(256)S(1)} all-reduce(f32[256]{0:T(256)S(1)} %multiply_reduce_fusion), channel_id=1, replica_groups=mesh['req'=2,'vocab'=64] {'vocab'}, use_global_device_ids=true, to_apply=%region_10.0 | all-reduce | flops 256 | bytes 2048 | tf_op jit(solution)/shard_map/psum | solution.py:63
  737.0 1.6 multiply_convert_fusion
  738.6 0.0 all-gather.5.cloned.1.call-update
  738.7 0.0 all-gather.3.cloned.1.call-done
  738.7 8.7 fusion.17
  747.4 54.3 %all-gather.5.cloned.1.call-done = bf16[7168,256]{1,0:T(8,128)(2,1)} async-done(((bf16[112,256]{1,0:T(8,128)(2,1)}), bf16[7168,256]{1,0:T(8,128)(2,1)}) %all-gather.5.cloned.1.call-update) | async-done | bytes 3670032 | tf_op jit(solution)/shard_map/all_gather | solution.py:71
  801.7 11.2 fusion.18
  813.0 0.0 copy-start.3
  813.0 0.0 copy-start.4
  813.0 174.7 %all-reduce.2 = (f32[256]{0:T(256)S(1)}, f32[256]{0:T(256)S(1)}) all-reduce(f32[256]{0:T(256)S(1)} %get-tuple-element.11, f32[256]{0:T(256)S(1)} %get-tuple-element.13), channel_id=1, replica_groups=mesh['req'=2,'vocab'=64] {'vocab'}, use_global_device_ids=true, to_apply=%region_3.0 | all-reduce | flops 512 | bytes 4096 | tf_op jit(solution)/shard_map/pmax | solution.py:78
  987.6 1.5 exponential_reduce_fusion
  989.1 0.3 exponential_reduce_fusion.1
  989.4 171.7 %all-reduce = (f32[256]{0:T(256)S(1)}, f32[256]{0:T(256)S(1)}) all-reduce(f32[256]{0:T(256)S(1)} %exponential_reduce_fusion.1, f32[256]{0:T(256)S(1)} %exponential_reduce_fusion), channel_id=1, replica_groups=mesh['req'=2,'vocab'=64] {'vocab'}, use_global_device_ids=true, to_apply=%region_5.0 | all-reduce | flops 512 | bytes 4096 | tf_op jit(solution)/shard_map/psum | solution.py:79
  1161.2 2.3 broadcast_subtract_fusion
  1163.5 0.0 copy-done.3
  1163.5 1.2 select_reduce_fusion
  1164.7 0.0 copy-done.4
  1164.7 0.2 convolution_bitcast_fusion
  1164.9 62.1 %psum.47 = f32[64]{0:T(128)} all-reduce(f32[64]{0:T(128)S(1)} %convolution_bitcast_fusion), channel_id=1, replica_groups=mesh['req'=2,'vocab'=64] {'req','vocab'}, use_global_device_ids=true, to_apply=%region_16.17 | all-reduce | flops 64 | bytes 512 | tf_op jit(solution)/shard_map/psum | solution.py:88
  (8 shorter events, 0.0 us)
Async XLA Ops:
  7.2 182.9 %copy-start = (bf16[112,7168]{1,0:T(8,128)(2,1)S(1)}, bf16[112,7168]{1,0:T(8,128)(2,1)}, u32[]{:S(2)}) copy-start(bf16[112,7168]{1,0:T(8,128)(2,1)} %param.18) | copy-start | bytes 4816900
  7.2 556.2 %reduce-scatter.4.cloned.1.call-start = ((), (), s32[]{:S(2)}) async-start(), calls=%async_computation.3 | async-start | bytes 7454720 | tf_op jit(solution)/shard_map/reduce_scatter | solution.py:52
  190.1 2.2 copy-start.1
  190.1 2.2 copy-start.2
  204.9 0.7 copy-start.5
  204.9 1.4 copy-start.6
  204.9 533.8 %all-gather.3.cloned.1.call-start = ((), (), s32[]{:S(2)}) async-start(), calls=%async_computation.1 | async-start | bytes 3727360 | tf_op jit(solution)/shard_map/all_gather | solution.py:48
  206.3 595.5 %all-gather.5.cloned.1.call-start = ((), (), s32[]{:S(2)}) async-start(), calls=%async_computation.2 | async-start | bytes 3727360 | tf_op jit(solution)/shard_map/all_gather | solution.py:71
  813.0 350.6 %copy-start.3 = (s32[256]{0:T(256)S(1)}, s32[256]{0:T(256)}, u32[]{:S(2)}) copy-start(s32[256]{0:T(256)} %param.20) | copy-start | bytes 3076
  813.0 351.7 %copy-start.4 = (s32[256]{0:T(256)S(1)}, s32[256]{0:T(256)}, u32[]{:S(2)}) copy-start(s32[256]{0:T(256)} %param.21) | copy-start | bytes 3076
Sparse Core Ops, SparseCore 0:
  205.0 358.2 reduce-scatter.3
  567.2 62.9 all-gather.2
  738.8 62.8 all-gather.4
where the time goes:
time: 1230 us
  blocking collectives  762 us (62%)
  waiting for transfers between devices  411 us (33%)
  matrix products  26.5 us (2%)
  between operations  13.8 us (1%)
    reduce_scatter x1, waiting for transfers between devices, per_device(): lax.psum_scatter(lax.dot_general(proj_embed, normed_embed, contract_cross...  357 us
    psum x1, blocking collectives, per_device(): lax.psum((jnp.sum(hidden_wide * hidden_wide, axis=1), jnp.sum(embed_wide...  180 us
    pmax x1, blocking collectives, per_device(): main_peak = lax.pmax(main_local, 'vocab')  175 us
    psum x1, blocking collectives, per_device(): draft_sq = lax.psum(jnp.sum(draft_state * draft_state, axis=0), 'vocab')  173 us
    psum x1, blocking collectives, per_device(): lax.psum(jnp.sum(jnp.exp(main_logits - main_peak[:, None]), axis=1), 'voc...  172 us
    psum x1, blocking collectives, per_device(): request_score = lax.psum(partial_score, ('req', 'vocab'))  62.1 us
    all_gather x1, waiting for transfers between devices, per_device(): lax.all_gather(normed_draft, 'vocab', axis=0, tiled=True)  54.3 us
  transfers between devices with their start and end apart: 3, of which 2 were waited for; matrix products, arithmetic and copies ran while one was open for 1% of the time, Pallas kernels for 0%

commit v1 on v0

v1 whole, which is shorter than its diff:
```python
import jax
import jax.numpy as jnp
from jax import lax
from jax.experimental import pallas as pl
from jax.experimental.pallas import tpu as pltpu
from jax.sharding import PartitionSpec as P

D = 7168
REQS = 64
SIDE = 4
FEAT = 112
ROWS = 256
VOC = 1024
QUART = D // SIDE
HALF = QUART // 2

epsilon = 1e-06
MESH = pl.DeviceIdType.MESH
DMA = pltpu.SemaphoreType.DMA
f32 = jnp.float32
bf16 = jnp.bfloat16
FIRST = (((0,), (0,)), ((), ()))

ORDERS = ((2, 1, 0), (0, 2, 1), (1, 0, 2))
H_PARTS = ((0, 48), (48, 32), (80, 32))
G_PARTS = ((0, 640), (640, 640), (1280, 512))


def coords():
    v = lax.axis_index("vocab")
    return (v // 16, (v // 4) % 4, v % 4)


def device(at, core):
    return (core, (at[0] * 4 + at[1]) * 4 + at[2])


def along(at, axis, step):
    moved = list(at)
    moved[axis] = (at[axis] + step) % 4
    return tuple(moved)


def picks(at, done):
    return tuple(pl.ds(0, 4) if a in done else at[a] for a in range(3))


class Gather:
    def __init__(self, view, order, send, recv, base):
        self.view, self.order, self.send, self.recv, self.base = view, order, send, recv, base

    def copies(self, phase):
        at, core = coords(), lax.axis_index("req")
        axis, done = self.order[phase], self.order[:phase]
        out = []
        for k in (1, 3, 2):
            here = self.view(picks(at, done))
            index = self.base + phase * 3 + k - 1
            out.append(
                pltpu.make_async_remote_copy(
                    src_ref=here,
                    dst_ref=here,
                    send_sem=self.send.at[index],
                    recv_sem=self.recv.at[index],
                    device_id=device(along(at, axis, k), core),
                    device_id_type=MESH,
                )
            )
        return out

    def start(self, phase):
        for copy in self.copies(phase):
            copy.start()

    def wait(self, phase):
        at, core = coords(), lax.axis_index("req")
        axis, done = self.order[phase], self.order[:phase]
        for k in (1, 3, 2):
            source = along(at, axis, 4 - k)
            there = self.view(picks(source, done))
            index = self.base + phase * 3 + k - 1
            pltpu.make_async_remote_copy(
                src_ref=there,
                dst_ref=there,
                send_sem=self.send.at[index],
                recv_sem=self.recv.at[index],
                device_id=device(along(at, axis, k), core),
                device_id_type=MESH,
            ).wait_recv()

    def wait_sends(self):
        for phase in range(3):
            for copy in self.copies(phase):
                copy.wait_send()


def turn(row):
    return jnp.broadcast_to(row, (128, row.shape[1])).T


def kernel(
    hid_ref, emb_ref, gains_ref, token_ref, request_ref, head_ref, pe_ref, ph_ref,
    main_ref, draft_ref, lse_ref, score_ref,
    head, small, gath, xe, xh, we, wh, part, recv, sq, gd, stats, score_buf,
    head_sem, own_sem,
    small_s, small_r, w_s, w_r, x_s, x_r, h_s, h_r, rs_s, rs_r, q_s, q_r, g_s, g_r, st_s, st_r, sc_s, sc_r,
):
    core = lax.axis_index("req")
    at = coords()
    x, y, z = at
    me32 = (x * 4 + y) * 2 + core

    barrier = pltpu.get_barrier_semaphore()

    def greet_plane(i, _):
        peer = (me32 + i) % 32
        pl.semaphore_signal(
            barrier, inc=1, device_id=device((peer // 8, (peer // 2) % 4, z), peer % 2), device_id_type=MESH
        )
        return 0

    lax.fori_loop(1, 32, greet_plane, 0)
    for k in (1, 2, 3):
        for c in (0, 1):
            pl.semaphore_signal(barrier, inc=1, device_id=device(along(at, 2, k), c), device_id_type=MESH)

    head_copies = [
        pltpu.make_async_copy(
            head_ref.at[pl.ds(i * QUART, QUART)], head.at[pl.ds(i * QUART, QUART)], head_sem.at[i]
        )
        for i in range(4)
    ]

    def columns(zz):
        return pl.ds(pl.multiple_of(zz * QUART + core * HALF, 128), HALF)

    own_copies = [
        pltpu.make_async_copy(pe_ref.at[:, columns(z)], we.at[z], own_sem.at[0]),
        pltpu.make_async_copy(ph_ref.at[:, columns(z)], wh.at[z], own_sem.at[1]),
    ]
    for copy in own_copies:
        copy.start()
    for copy in head_copies:
        copy.start()

    hid = hid_ref[...].astype(f32)
    emb = emb_ref[...].astype(f32)
    gains = gains_ref[...]
    block = jnp.concatenate(
        [
            jnp.sum(hid * hid, axis=0, keepdims=True),
            jnp.sum(emb * emb, axis=0, keepdims=True),
            jnp.concatenate([gains[3:4], gains[3:4]], axis=1),
            jnp.zeros((5, ROWS), f32),
        ],
        axis=0,
    )
    small[x, y, z] = block
    pl.semaphore_wait(barrier, 37)

    small_gather = Gather(lambda s: small.at[s], (2, 1, 0), small_s, small_r, 0)
    small_gather.start(0)

    def w_copies(k):
        to = along(at, 2, k)
        return [
            pltpu.make_async_remote_copy(
                src_ref=src.at[:, columns(to[2])],
                dst_ref=dst.at[z],
                send_sem=w_s.at[j, k - 1],
                recv_sem=w_r.at[j, k - 1],
                device_id=device(to, core),
                device_id_type=MESH,
            )
            for j, (src, dst) in enumerate(((pe_ref, we), (ph_ref, wh)))
        ]

    for k in (1, 3, 2):
        for copy in w_copies(k):
            copy.start()

    small_gather.wait(0)
    small_gather.start(1)
    final_gain = turn(gains[0:1])[:FEAT, :1]
    hidden_gain = turn(gains[1:2])[:FEAT, :1]
    embed_gain = turn(gains[2:3])[:FEAT, :1]
    small_gather.wait(1)
    small_gather.start(2)
    small_gather.wait(2)

    squares = jnp.sum(small[...].reshape(64, 8, ROWS), axis=0)
    hid_scale = lax.rsqrt(squares[0:1] / D + epsilon)
    emb_scale = lax.rsqrt(squares[1:2] / D + epsilon)
    gath[x, y, z] = (hid * hid_scale * final_gain).astype(bf16)
    mine = pl.ds(pl.multiple_of(core * ROWS, 128), ROWS)
    xe[z, :, mine] = (emb * emb_scale * embed_gain).astype(bf16)
    xh[z, :, mine] = (hid * hid_scale * hidden_gain).astype(bf16)

    def x_copies():
        out = []
        for k in range(4):
            for dc in (0, 1):
                if k == 0 and dc == 0:
                    continue
                for j, buf in enumerate((xe, xh)):
                    out.append(
                        pltpu.make_async_remote_copy(
                            src_ref=buf.at[z, :, mine],
                            dst_ref=buf.at[z, :, mine],
                            send_sem=x_s.at[j, k * 2 + dc],
                            recv_sem=x_r.at[j, k * 2 + dc],
                            device_id=device(along(at, 2, k), (core + dc) % 2),
                            device_id_type=MESH,
                        )
                    )
        return out

    def x_waits():
        for k in range(4):
            for dc in (0, 1):
                if k == 0 and dc == 0:
                    continue
                lanes = pl.ds(pl.multiple_of(((core + dc) % 2) * ROWS, 128), ROWS)
                for j, buf in enumerate((xe, xh)):
                    ref = buf.at[(z + 4 - k) % 4, :, lanes]
                    pltpu.make_async_remote_copy(
                        src_ref=ref,
                        dst_ref=ref,
                        send_sem=x_s.at[j, k * 2 + dc],
                        recv_sem=x_r.at[j, k * 2 + dc],
                        device_id=device(along(at, 2, k), (core + dc) % 2),
                        device_id_type=MESH,
                    ).wait_recv()

    for copy in x_copies():
        copy.start()

    h_gathers = [
        Gather(
            lambda s, r=r, n=n: gath.at[s + (pl.ds(r, n), slice(None))], order, h_s, h_r, 9 * p
        )
        for p, (order, (r, n)) in enumerate(zip(ORDERS, H_PARTS))
    ]
    for gather in h_gathers:
        gather.start(0)

    draft_gain = jnp.concatenate(
        [small[z, yy, zz, 2:3, :FEAT] for yy in range(4) for zz in range(4)], axis=1
    )
    token = turn(token_ref[...].astype(f32))
    base = (lax.axis_index("vocab") * VOC).astype(f32)

    for copy in own_copies:
        copy.wait()
    for k in (1, 3, 2):
        for j, dst in enumerate((we, wh)):
            ref = dst.at[(z + 4 - k) % 4]
            pltpu.make_async_remote_copy(
                src_ref=ref,
                dst_ref=ref,
                send_sem=w_s.at[j, k - 1],
                recv_sem=w_r.at[j, k - 1],
                device_id=device(along(at, 2, k), core),
                device_id_type=MESH,
            ).wait_recv()
    x_waits()

    def project(c, _):
        lanes = pl.ds(pl.multiple_of(c * ROWS, 128), ROWS)
        got = lax.dot_general(
            xe[:, :, lanes].reshape(4 * FEAT, ROWS), we[...].reshape(4 * FEAT, HALF), FIRST,
            preferred_element_type=f32,
        ) + lax.dot_general(
            xh[:, :, lanes].reshape(4 * FEAT, ROWS), wh[...].reshape(4 * FEAT, HALF), FIRST,
            preferred_element_type=f32,
        )
        part[:, c] = got.reshape(16, 16, HALF)
        return 0

    lax.fori_loop(0, 2, project, 0)

    def share(i):
        peer = (me32 + i) % 32
        return pltpu.make_async_remote_copy(
            src_ref=part.at[peer // 2, peer % 2],
            dst_ref=recv.at[me32],
            send_sem=rs_s.at[i],
            recv_sem=rs_r.at[i],
            device_id=device((peer // 8, (peer // 2) % 4, z), peer % 2),
            device_id_type=MESH,
        )

    def send_share(i, _):
        share(i).start()
        return 0

    lax.fori_loop(1, 32, send_share, 0)
    recv[me32] = part[me32 // 2, core]

    for gather in h_gathers:
        gather.wait(0)
        gather.start(1)
    for gather in h_gathers:
        gather.wait(1)
        gather.start(2)

    def wait_share(i, _):
        ref = recv.at[(me32 + 32 - i) % 32]
        peer = (me32 + i) % 32
        pltpu.make_async_remote_copy(
            src_ref=ref,
            dst_ref=ref,
            send_sem=rs_s.at[i],
            recv_sem=rs_r.at[i],
            device_id=device((peer // 8, (peer // 2) % 4, z), peer % 2),
            device_id_type=MESH,
        ).wait_recv()
        return 0

    lax.fori_loop(1, 32, wait_share, 0)

    def add(i, halves):
        return (halves[0] + recv[2 * i], halves[1] + recv[2 * i + 1])

    left, right = lax.fori_loop(1, 16, add, (recv[0], recv[1]))
    state = jnp.concatenate([left, right], axis=1)
    sq[z] = jnp.broadcast_to(jnp.sum(state * state, axis=1, keepdims=True), (16, 128))

    def q_copy(k, source):
        ref = sq.at[source]
        return pltpu.make_async_remote_copy(
            src_ref=ref,
            dst_ref=ref,
            send_sem=q_s.at[k - 1],
            recv_sem=q_r.at[k - 1],
            device_id=device(along(at, 2, k), core),
            device_id_type=MESH,
        )

    for k in (1, 3, 2):
        q_copy(k, z).start()
    for copy in head_copies:
        copy.wait()
    for k in (1, 3, 2):
        q_copy(k, (z + 4 - k) % 4).wait_recv()
    total = jnp.sum(sq[...], axis=0)[:, :1]
    gd[z, x, y] = (state * lax.rsqrt(total / D + epsilon) * draft_gain).astype(bf16)

    g_gathers = [
        Gather(
            lambda s, c=c, n=n: gd.at[s[2], s[0], s[1], :, pl.ds(c, n)], order, g_s, g_r, 9 * p
        )
        for p, (order, (c, n)) in enumerate(zip(ORDERS, G_PARTS))
    ]
    for gather in g_gathers:
        gather.start(0)

    for gather in h_gathers:
        gather.wait(2)

    def main_dot(q):
        got = lax.dot_general(
            gath[q].reshape(QUART, ROWS), head[pl.ds(q * QUART, QUART)], FIRST, preferred_element_type=f32
        )
        main_ref[...] = got if q == 0 else main_ref[...] + got

    main_dot(0)
    for gather in g_gathers:
        gather.wait(0)
        gather.start(1)
    main_dot(1)
    for gather in g_gathers:
        gather.wait(1)
        gather.start(2)
    main_dot(2)
    main_dot(3)

    def local_stats(ref):
        logits = ref[...]
        top = jnp.max(logits, axis=1, keepdims=True)
        return top, jnp.sum(jnp.exp(logits - top), axis=1, keepdims=True)

    main_top, main_sum = local_stats(main_ref)
    column = lax.broadcasted_iota(jnp.int32, (ROWS, VOC), 1).astype(f32) + base
    picked = jnp.sum(jnp.where(column == token[:, :1], main_ref[...], 0.0), axis=1, keepdims=True)

    for gather in g_gathers:
        gather.wait(2)

    def draft_dot(q):
        got = jnp.dot(
            gd[q].reshape(ROWS, QUART), head[pl.ds(q * QUART, QUART)], preferred_element_type=f32
        )
        draft_ref[...] = got if q == 0 else draft_ref[...] + got

    for q in range(4):
        draft_dot(q)
    draft_top, draft_sum = local_stats(draft_ref)

    lane = lax.broadcasted_iota(jnp.int32, (ROWS, 128), 1)
    packed = jnp.zeros((ROWS, 128), f32)
    for i, value in enumerate((main_top, main_sum, picked, draft_top, draft_sum)):
        packed = jnp.where(lane == i, value, packed)
    mine8 = packed.T[:8]

    def merge(tops, sums):
        top = jnp.max(tops, axis=0, keepdims=True)
        return top, jnp.sum(sums * jnp.exp(tops - top), axis=0, keepdims=True)

    for phase, axis in enumerate((2, 1, 0)):
        stats[phase, at[axis]] = mine8

        def st_copy(k, source):
            ref = stats.at[phase, source]
            return pltpu.make_async_remote_copy(
                src_ref=ref,
                dst_ref=ref,
                send_sem=st_s.at[phase * 3 + k - 1],
                recv_sem=st_r.at[phase * 3 + k - 1],
                device_id=device(along(at, axis, k), core),
                device_id_type=MESH,
            )

        for k in (1, 3, 2):
            st_copy(k, at[axis]).start()
        for k in (1, 3, 2):
            st_copy(k, (at[axis] + 4 - k) % 4).wait_recv()
        got = stats[phase]
        m_top, m_sum = merge(got[:, 0], got[:, 1])
        d_top, d_sum = merge(got[:, 3], got[:, 4])
        pick = jnp.sum(got[:, 2], axis=0, keepdims=True)
        mine8 = jnp.concatenate([m_top, m_sum, pick, d_top, d_sum, jnp.zeros((3, ROWS), f32)], axis=0)
        for k in (1, 3, 2):
            st_copy(k, at[axis]).wait_send()

    m_lse = m_top + jnp.log(m_sum)
    d_lse = d_top + jnp.log(d_sum)
    lse_ref[...] = jnp.concatenate([m_lse, d_lse, jnp.zeros((6, ROWS), f32)], axis=0)

    member = lax.broadcasted_iota(jnp.int32, (REQS, ROWS), 0) == request_ref[...]
    partial = jnp.sum(jnp.where(member, pick - m_lse, 0.0), axis=1, keepdims=True)
    score_buf[core] = jnp.broadcast_to(partial, (REQS, 128))

    def sc_copy(source):
        ref = score_buf.at[source]
        return pltpu.make_async_remote_copy(
            src_ref=ref,
            dst_ref=ref,
            send_sem=sc_s,
            recv_sem=sc_r,
            device_id=device(at, 1 - core),
            device_id_type=MESH,
        )

    sc_copy(core).start()

    small_gather.wait_sends()
    for k in (1, 3, 2):
        for copy in w_copies(k):
            copy.wait_send()
        q_copy(k, z).wait_send()
    for copy in x_copies():
        copy.wait_send()
    for gather in h_gathers + g_gathers:
        gather.wait_sends()

    def wait_sent(i, _):
        share(i).wait_send()
        return 0

    lax.fori_loop(1, 32, wait_sent, 0)
    sc_copy(1 - core).wait_recv()
    score_ref[...] = score_buf[0] + score_buf[1]
    sc_copy(core).wait_send()


def per_device(
    hidden,
    next_embedding,
    final_gain,
    hidden_gain,
    embed_gain,
    draft_gain,
    head_weight,
    proj_embed,
    proj_hidden,
    token_ids,
    row_request,
):
    gains = jnp.stack([final_gain, hidden_gain, embed_gain, draft_gain]).astype(f32)
    gains = jnp.pad(gains, ((0, 4), (0, 128 - FEAT)))
    vmem = pl.BlockSpec(memory_space=pltpu.VMEM)
    hbm = pl.BlockSpec(memory_space=pl.ANY)
    main, draft, lse, score = pl.pallas_call(
        kernel,
        name="heads",
        out_shape=(
            jax.ShapeDtypeStruct((ROWS, VOC), f32),
            jax.ShapeDtypeStruct((ROWS, VOC), f32),
            jax.ShapeDtypeStruct((8, ROWS), f32),
            jax.ShapeDtypeStruct((REQS, 128), f32),
        ),
        in_specs=[vmem] * 5 + [hbm] * 3,
        out_specs=(vmem,) * 4,
        scratch_shapes=[
            pltpu.VMEM((D, VOC), bf16),
            pltpu.VMEM((4, 4, 4, 8, ROWS), f32),
            pltpu.VMEM((4, 4, 4, FEAT, ROWS), bf16),
            pltpu.VMEM((4, FEAT, 2 * ROWS), bf16),
            pltpu.VMEM((4, FEAT, 2 * ROWS), bf16),
            pltpu.VMEM((4, FEAT, HALF), bf16),
            pltpu.VMEM((4, FEAT, HALF), bf16),
            pltpu.VMEM((16, 2, 16, HALF), f32),
            pltpu.VMEM((32, 16, HALF), f32),
            pltpu.VMEM((4, 16, 128), f32),
            pltpu.VMEM((4, 4, 4, 16, QUART), bf16),
            pltpu.VMEM((3, 4, 8, ROWS), f32),
            pltpu.VMEM((2, REQS, 128), f32),
            DMA((4,)),
            DMA((2,)),
            DMA((9,)),
            DMA((9,)),
            DMA((2, 3)),
            DMA((2, 3)),
            DMA((2, 8)),
            DMA((2, 8)),
            DMA((27,)),
            DMA((27,)),
            DMA((32,)),
            DMA((32,)),
            DMA((3,)),
            DMA((3,)),
            DMA((27,)),
            DMA((27,)),
            DMA((9,)),
            DMA((9,)),
            DMA,
            DMA,
        ],
        compiler_params=pltpu.CompilerParams(
            collective_id=0, has_side_effects=True, vmem_limit_bytes=48 * 2**20
        ),
        cost_estimate=pl.CostEstimate(flops=8_300_000_000, bytes_accessed=20_000_000, transcendentals=600_000),
    )(
        hidden.T,
        next_embedding.T,
        gains,
        token_ids[None, :],
        row_request[None, :],
        head_weight,
        proj_embed,
        proj_hidden,
    )
    return (main - lse[0][:, None], draft - lse[1][:, None], score[:, 0])


def solution(mesh):
    return jax.shard_map(
        per_device,
        mesh=mesh,
        in_specs=(
            P("req", "vocab"),
            P("req", "vocab"),
            P("vocab"),
            P("vocab"),
            P("vocab"),
            P("vocab"),
            P(None, "vocab"),
            P("vocab", None),
            P("vocab", None),
            P("req"),
            P("req"),
        ),
        out_specs=(P("req", "vocab"), P("req", "vocab"), P()),
        check_vma=False,
    )
```

time: 1230 us -> 148 us (0.12)
  blocking collectives: 762 us -> 0 us
  waiting for transfers between devices: 411 us -> 0 us
  Pallas kernels: 0 us -> 137 us
  matrix products: 26.5 us -> 0 us
  between operations: 13.8 us -> 0.66 us
    psum x4 -> x0, blocking collectives: 587 us -> none  [the longest x1 180 us: per_device(): lax.psum((jnp.sum(hidden_wide * hidden_wide, axis=1), jnp.sum(embed_wide...]
    reduce_scatter x1 -> x0, waiting for transfers between devices: 357 us -> none  [per_device(): lax.psum_scatter(lax.dot_general(proj_embed, normed_embed, contract_cross...]
    pmax x1 -> x0, blocking collectives: 175 us -> none  [per_device(): main_peak = lax.pmax(main_local, 'vocab')]
    pallas_call x0 -> x1, Pallas kernels: none -> 137 us  [per_device(): pl.pallas_call(kernel, name='heads', out_shape=(jax.ShapeDtypeStruct((ROW...]
    all_gather x2 -> x0, waiting for transfers between devices: 54.4 us -> none  [the longest x1 54.3 us: per_device(): lax.all_gather(normed_draft, 'vocab', axis=0, tiled=True)]
    dot_general x5 -> x0, matrix products: 26.5 us -> none  [the longest x1 11.2 us: per_device(): lax.dot_general(lax.all_gather(normed_draft, 'vocab', axis=0, tiled=True)...]
  transfers between devices with their start and end apart: 3 -> 0, of which waited for: 2 -> 0; matrix products, arithmetic and copies ran while one was open for 1% -> 0% of each run, Pallas kernels for 0% -> 0%
where the time goes in v1:
time: 148 us; the launch traced here: 147 us
  Pallas kernels  137 us (93%)
  local copies, waits for them, and re-layouts  6.46 us (4%)
  other arithmetic  2.24 us (2%)
    pallas_call x1, Pallas kernels, per_device(): pl.pallas_call(kernel, name='heads', out_shape=(jax.ShapeDtypeStruct((ROW...  137 us
    unnamed x12, local copies, waits for them, and re-layouts  5.83 us

profile of v1, /device:TPU:0, one launch (start us, length us, event | category | flops | bytes accessed | tf_op | source)
XLA Modules:
  0.0 146.8 jit_solution(15940772524527105411)
XLA Ops:
  0.6 0.7 fusion.9.gains_ref
  1.3 0.0 copy-start
  1.4 1.4 copy-done
  2.8 0.0 copy-start.1
  2.8 1.4 copy-done.1
  4.2 0.0 copy-start.2
  4.2 0.8 copy-done.2
  5.0 0.0 copy-start.3
  5.0 0.8 copy-done.3
  5.8 0.0 copy-start.4
  5.8 0.7 copy-done.4
  6.5 0.0 copy-start.5
  6.5 0.7 copy-done.5
  7.2 137.4 %heads.1 = (f32[256,1024]{1,0:T(8,128)S(1)}, f32[256,1024]{1,0:T(8,128)S(1)}, f32[8,256]{1,0:T(8,128)S(1)}, f32[64,128]{1,0:T(8,128)S(1)}) custom-call(bf16[112,256]{1,0:T(8,128)(2,1)S(1)} %bitcast.10, bf16[112,256]{1,0:T(8,128)(2,1)S(1)} %bitcast.11, f32[8,128]{1,0:T(8,128)S(1)} %fusion.9.gains_ref, s32[1,256]{1,0:T(1,128)S(1)} %bitcast.12, ...), custom_call_target="tpu_custom_call" | custom-call | flops 8300000256 | bytes 20000000 | tf_op jit(solution)/shard_map/heads/pallas_call | solution.py:494
  144.6 0.6 slice_reduce_fusion
  145.3 1.5 %broadcast_subtract_fusion = (f32[256,1024]{1,0:T(8,128)}, f32[256,1024]{1,0:T(8,128)}) fusion(f32[256,1024]{1,0:T(8,128)S(1)} %get-tuple-element.9, f32[256]{0:T(256)S(1)} %bitcast.14, f32[256,1024]{1,0:T(8,128)S(1)} %get-tuple-element.7, f32[256]{0:T(256)S(1)} %bitcast.15), kind=kLoop, calls=%fused_computation | loop fusion | flops 524288 | bytes 4196352 | tf_op jit(solution)/shard_map/sub | solution.py:554
  (1 shorter events, 0.0 us)
Async XLA Ops:
  1.3 1.4 copy-start
  2.8 1.4 copy-start.1
  4.2 0.8 copy-start.2
  5.0 0.8 copy-start.3
  5.8 0.7 copy-start.4
  6.5 0.7 copy-start.5

commit v2 on v0

v2 whole, which is shorter than its diff:
```python
import jax
import jax.numpy as jnp
from jax import lax
from jax.experimental import pallas as pl
from jax.experimental.pallas import tpu as pltpu
from jax.sharding import PartitionSpec as P

D = 7168
REQS = 64
SIDE = 4
FEAT = 112
ROWS = 256
VOC = 1024
QUART = D // SIDE
HALF = QUART // 2

epsilon = 1e-06
MESH = pl.DeviceIdType.MESH
DMA = pltpu.SemaphoreType.DMA
f32 = jnp.float32
bf16 = jnp.bfloat16
FIRST = (((0,), (0,)), ((), ()))

H_ORDERS = ((2, 0, 1), (2, 1, 0), (0, 1, 2))
G_ORDERS = ((2, 1, 0), (0, 2, 1), (1, 0, 2))
H_PARTS = ((0, 80, 0, 128), (0, 80, 128, 128), (80, 32, 0, 256))
G_PARTS = ((0, 640), (640, 640), (1280, 512))

OTHERS = pl.ds(1, 3)
STEPS = {
    "0a": (0, (0, 0, 0)),
    "0b": (1, (0, 0, 0)),
    "0c": (2, (0, 0, 0)),
    "1b": (1, (OTHERS, 0, 0)),
    "1c": (2, (OTHERS, 0, 0)),
    "2c": (2, (0, OTHERS, 0)),
    "3c": (2, (OTHERS, OTHERS, 0)),
}


def coords():
    v = lax.axis_index("vocab")
    return (v // 16, (v // 4) % 4, v % 4)


def device(at, core):
    return (core, (at[0] * 4 + at[1]) * 4 + at[2])


def along(at, axis, step):
    moved = list(at)
    moved[axis] = (at[axis] + step) % 4
    return tuple(moved)


class Gather:
    def __init__(self, waits, name, view, order, send, recv, base):
        self.waits, self.name, self.view, self.order = waits, name, view, order
        self.sems, self.base = (send, recv), base

    def copy(self, step, k, landed):
        place, blocks = STEPS[step]
        there = list(blocks)
        there[place] = 4 - k
        index = self.base + list(STEPS).index(step) * 3 + k - 1
        src, dst = (self.view(tuple(b[self.order.index(a)] for a in range(3))) for b in (blocks, there))
        return pltpu.make_async_remote_copy(
            src_ref=dst if landed else src,
            dst_ref=dst,
            send_sem=self.sems[0].at[index],
            recv_sem=self.sems[1].at[index],
            device_id=device(along(coords(), self.order[place], k), lax.axis_index("req")),
            device_id_type=MESH,
        )

    def start(self, *steps):
        for step in steps:
            self.waits.send([self.copy(step, k, False) for k in (1, 3, 2)])

            def wait(step=step):
                for k in (1, 3, 2):
                    self.copy(step, k, True).wait_recv()

            self.waits.expect(self.name + step, wait)

    def wait(self, *steps):
        for step in steps:
            self.waits.receive(self.name + step)


def turn(row):
    return jnp.broadcast_to(row, (128, row.shape[1])).T


class Waits:
    def __init__(self):
        self.receives, self.sends = {}, []

    def send(self, copies):
        for copy in copies:
            copy.start()
        self.sends += copies

    def expect(self, name, wait):
        self.receives[name] = wait

    def receive(self, name):
        self.receives.pop(name)()

    def finish(self):
        for name in list(self.receives):
            self.receive(name)
        for copy in self.sends:
            copy.wait_send()


def kernel(
    hid_hbm, emb_hbm, gains_ref, token_hbm, request_hbm, head_ref, pe_ref, ph_ref,
    main_ref, draft_ref, lse_ref, score_ref,
    emb_ref, token_ref, request_ref,
    head, small, gath, normed, xe, xh, we, wh, part, got1, sum1, got2, sq, gd, acc, stats, score_buf,
    head_sem, own_sem,
    small_s, small_r, w_s, w_r, x_s, x_r, h_s, h_r, r1_s, r1_r, r2_s, r2_r, q_s, q_r, g_s, g_r,
    st_s, st_r, sc_s, sc_r,
):
    core = lax.axis_index("req")
    at = coords()
    x, y, z = at
    waits = Waits()

    def columns(zz):
        return pl.ds(pl.multiple_of(zz * QUART + core * HALF, 128), HALF)

    row_copies = [
        pltpu.make_async_copy(hid_hbm, gath.at[0, 0, 0], own_sem.at[2]),
        pltpu.make_async_copy(emb_hbm, emb_ref, own_sem.at[3]),
    ]
    id_copies = [
        pltpu.make_async_copy(token_hbm, token_ref, own_sem.at[4]),
        pltpu.make_async_copy(request_hbm, request_ref, own_sem.at[5]),
    ]
    own_copies = [
        pltpu.make_async_copy(pe_ref.at[:, columns(z)], we.at[z], own_sem.at[0]),
        pltpu.make_async_copy(ph_ref.at[:, columns(z)], wh.at[z], own_sem.at[1]),
    ]
    head_copies = [
        pltpu.make_async_copy(
            head_ref.at[pl.ds(i * QUART, QUART)], head.at[pl.ds(i * QUART, QUART)], head_sem.at[i]
        )
        for i in range(4)
    ]
    for copy in row_copies:
        copy.start()

    barrier = pltpu.get_barrier_semaphore()
    partners = [device(at, 1 - core)] + [
        device(along(at, axis, k), c) for axis in (2, 1, 0) for k in (1, 2, 3) for c in (0, 1)
    ]
    for partner in partners:
        pl.semaphore_signal(barrier, inc=1, device_id=partner, device_id_type=MESH)
    for copy in own_copies + id_copies + head_copies:
        copy.start()

    for copy in row_copies:
        copy.wait()
    hid = gath[0, 0, 0].astype(f32)
    emb = emb_ref[...].astype(f32)
    gains = gains_ref[...]

    def wide(row):
        return jnp.concatenate([row, row], axis=1)

    small[0, 0, 0] = jnp.concatenate(
        [
            jnp.sum(hid * hid, axis=0, keepdims=True),
            jnp.sum(emb * emb, axis=0, keepdims=True),
            wide(gains[3:4]),
            wide(gains[0:1]),
            jnp.zeros((4, ROWS), f32),
        ],
        axis=0,
    )
    pl.semaphore_wait(barrier, len(partners))

    def small_copy(phase, k, landed):
        blocks = [(0, 0, 0), (0, 0, pl.ds(0, 4)), (0, pl.ds(0, 4), pl.ds(0, 4))][phase]
        there = list(blocks)
        there[2 - phase] = 4 - k
        return pltpu.make_async_remote_copy(
            src_ref=small.at[tuple(there) if landed else blocks],
            dst_ref=small.at[tuple(there)],
            send_sem=small_s.at[phase * 3 + k - 1],
            recv_sem=small_r.at[phase * 3 + k - 1],
            device_id=device(along(at, 2 - phase, k), core),
            device_id_type=MESH,
        )

    def small_start(phase):
        waits.send([small_copy(phase, k, False) for k in (1, 3, 2)])

    def small_wait(phase):
        for k in (1, 3, 2):
            small_copy(phase, k, True).wait_recv()

    small_start(0)

    ha, hb, hc = [
        Gather(
            waits,
            "h%d" % p,
            lambda s, r=r, n=n, c=c, m=m: gath.at[s + (pl.ds(r, n), pl.ds(c, m))],
            order,
            h_s,
            h_r,
            21 * p,
        )
        for p, (order, (r, n, c, m)) in enumerate(zip(H_ORDERS, H_PARTS))
    ]
    ha.start("0a")
    hb.start("0a")
    hc.start("0a")

    w_pairs = ((pe_ref, we), (ph_ref, wh))

    def w_copy(k, j, src, dst):
        return pltpu.make_async_remote_copy(
            src_ref=src,
            dst_ref=dst,
            send_sem=w_s.at[j, k - 1],
            recv_sem=w_r.at[j, k - 1],
            device_id=device(along(at, 2, k), core),
            device_id_type=MESH,
        )

    for k in (1, 3, 2):
        waits.send([w_copy(k, j, src.at[:, columns((z + k) % 4)], dst.at[z]) for j, (src, dst) in enumerate(w_pairs)])

    def w_wait():
        for k in (1, 3, 2):
            for j, (_, dst) in enumerate(w_pairs):
                ref = dst.at[(z + 4 - k) % 4]
                w_copy(k, j, ref, ref).wait_recv()

    waits.expect("w", w_wait)

    small_wait(0)
    small_start(1)
    ha.start("0b", "0c")
    hb.start("0b", "0c")
    hc.start("0b")
    hidden_gain = turn(gains[1:2])[:FEAT, :1]
    embed_gain = turn(gains[2:3])[:FEAT, :1]
    small_wait(1)
    small_start(2)
    ha.wait("0a")
    hb.wait("0a")
    ha.start("1b")
    hb.start("1b")
    hc.wait("0a")
    hc.start("1b")
    small_wait(2)

    squares = jnp.sum(small[...].reshape(64, 8, ROWS), axis=0)
    hid_scale = lax.rsqrt(squares[0:1] / D + epsilon)
    emb_scale = lax.rsqrt(squares[1:2] / D + epsilon)
    mine = pl.ds(pl.multiple_of(core * ROWS, 128), ROWS)
    xe[z, :, mine] = (emb * emb_scale * embed_gain).astype(bf16)
    xh[z, :, mine] = (hid * hid_scale * hidden_gain).astype(bf16)

    line = [(k, dc) for k in range(4) for dc in (0, 1)][1:]

    def x_copy(k, dc, j, ref):
        return pltpu.make_async_remote_copy(
            src_ref=ref,
            dst_ref=ref,
            send_sem=x_s.at[j, k * 2 + dc],
            recv_sem=x_r.at[j, k * 2 + dc],
            device_id=device(along(at, 2, k), (core + dc) % 2),
            device_id_type=MESH,
        )

    for k, dc in line:
        waits.send([x_copy(k, dc, j, buf.at[z, :, mine]) for j, buf in enumerate((xe, xh))])

    def x_wait():
        for k, dc in line:
            lanes = pl.ds(pl.multiple_of(((core + dc) % 2) * ROWS, 128), ROWS)
            for j, buf in enumerate((xe, xh)):
                x_copy(k, dc, j, buf.at[(z + 4 - k) % 4, :, lanes]).wait_recv()

    waits.expect("x", x_wait)

    ha.start("1c")
    hb.start("1c")
    ha.wait("0b")
    hb.wait("0b")
    ha.start("2c")
    hb.start("2c")
    ha.wait("1b")
    ha.start("3c")
    hb.wait("1b")
    hb.start("3c")

    for copy in own_copies + id_copies:
        copy.wait()
    draft_gain = jnp.concatenate(
        [
            small[(z + 4 - x) % 4, (yy + 4 - y) % 4, (zz + 4 - z) % 4, 2:3, :FEAT]
            for yy in range(4)
            for zz in range(4)
        ],
        axis=1,
    )
    token = turn(token_ref[...].astype(f32))
    base = (lax.axis_index("vocab") * VOC).astype(f32)

    waits.receive("w")
    waits.receive("x")

    for c in (0, 1):
        lanes = pl.ds(c * ROWS, ROWS)
        rows = lax.dot_general(
            xe[:, :, lanes].reshape(4 * FEAT, ROWS), we[...].reshape(4 * FEAT, HALF), FIRST,
            preferred_element_type=f32,
        ) + lax.dot_general(
            xh[:, :, lanes].reshape(4 * FEAT, ROWS), wh[...].reshape(4 * FEAT, HALF), FIRST,
            preferred_element_type=f32,
        )
        part[:, :, c] = rows.reshape(4, 4, 2, 8, HALF)

    def r1_copy(half, k):
        to = (at[half] + k) % 4
        src = part.at[to, :, :, 0] if half == 0 else part.at[:, to, :, 1]
        return pltpu.make_async_remote_copy(
            src_ref=src,
            dst_ref=got1.at[half, k - 1],
            send_sem=r1_s.at[half * 3 + k - 1],
            recv_sem=r1_r.at[half * 3 + k - 1],
            device_id=device(along(at, half, k), core),
            device_id_type=MESH,
        )

    def r2_copy(half, k, dc):
        to = (core + dc) % 2
        axis = 1 - half
        return pltpu.make_async_remote_copy(
            src_ref=sum1.at[half, (at[axis] + k) % 4, to],
            dst_ref=got2.at[half, k * 2 + dc],
            send_sem=r2_s.at[half * 8 + k * 2 + dc],
            recv_sem=r2_r.at[half * 8 + k * 2 + dc],
            device_id=device(along(at, axis, k), to),
            device_id_type=MESH,
        )

    for k in (1, 3, 2):
        waits.send([r1_copy(0, k), r1_copy(1, k)])
    hc.wait("0b")
    hc.wait("1b")
    hc.start("0c", "1c", "2c", "3c")
    for half in (0, 1):
        own = part[x, :, :, 0] if half == 0 else part[:, y, :, 1]
        for k in (1, 3, 2):
            r1_copy(half, k).wait_recv()
            own = own + got1[half, k - 1]
        sum1[half] = own
        waits.send([r2_copy(half, k, dc) for k, dc in line])

    state_halves = []
    for half in (0, 1):
        for k, dc in line:
            r2_copy(half, k, dc).wait_recv()
        same = sum1[half, at[1 - half], core]
        for k in (1, 2, 3):
            same = same + got2[half, k * 2]
        other = got2[half, 1] + got2[half, 3] + got2[half, 5] + got2[half, 7]
        state_halves.append(
            jnp.concatenate(
                [jnp.where(core == 0, same, other), jnp.where(core == 0, other, same)], axis=1
            )
        )
    state = jnp.concatenate(state_halves, axis=0)
    sq[z] = jnp.broadcast_to(jnp.sum(state * state, axis=1, keepdims=True), (16, 128))

    def q_copy(k, source):
        ref = sq.at[source]
        return pltpu.make_async_remote_copy(
            src_ref=ref,
            dst_ref=ref,
            send_sem=q_s.at[k - 1],
            recv_sem=q_r.at[k - 1],
            device_id=device(along(at, 2, k), core),
            device_id_type=MESH,
        )

    waits.send([q_copy(k, z) for k in (1, 3, 2)])
    for copy in head_copies:
        copy.wait()
    for k in (1, 3, 2):
        q_copy(k, (z + 4 - k) % 4).wait_recv()
    total = jnp.sum(sq[...], axis=0)[:, :1]
    gd[0, 0, 0] = (state * lax.rsqrt(total / D + epsilon) * draft_gain).astype(bf16)

    gs = [
        Gather(waits, "g%d" % p, lambda s, c=c, n=n: gd.at[s + (slice(None), pl.ds(c, n))], order, g_s, g_r, 21 * p)
        for p, (order, (c, n)) in enumerate(zip(G_ORDERS, G_PARTS))
    ]
    for g in gs:
        g.start("0a")
    for g in gs:
        g.start("0b")
    for g in gs:
        g.start("0c")
    for g in gs:
        g.wait("0a")
        g.start("1b")
    for g in gs:
        g.wait("0b")
        g.start("1c", "2c")
    for h in (ha, hb):
        h.wait("0c", "1c", "2c", "3c")
    hc.wait("0c", "1c", "2c", "3c")

    def norm(xr, _):
        gain = small[xr].reshape(16, 8, ROWS)[:, 3, :128].T
        for yr in range(4):
            for zr in range(4):
                block = gath[xr, yr, zr].astype(f32) * hid_scale * gain[:FEAT, yr * 4 + zr : yr * 4 + zr + 1]
                normed[(x + xr) % 4, (y + yr) % 4, (z + zr) % 4] = block.astype(bf16)
        return 0

    lax.fori_loop(0, 4, norm, 0)
    for g in gs:
        g.wait("1b")
        g.start("3c")

    def main_dot(q):
        rows = lax.dot_general(
            normed[q].reshape(QUART, ROWS), head[pl.ds(q * QUART, QUART)], FIRST, preferred_element_type=f32
        )
        main_ref[...] = rows if q == 0 else main_ref[...] + rows

    for q in range(4):
        main_dot(q)

    def local_stats(ref):
        logits = ref[...]
        top = jnp.max(logits, axis=1, keepdims=True)
        return top, jnp.sum(jnp.exp(logits - top), axis=1, keepdims=True)

    main_top, main_sum = local_stats(main_ref)
    column = lax.broadcasted_iota(jnp.int32, (ROWS, VOC), 1).astype(f32) + base
    picked = jnp.sum(jnp.where(column == token[:, :1], main_ref[...], 0.0), axis=1, keepdims=True)

    for g in gs:
        g.wait("0c", "1c", "2c", "3c")

    for zr in range(4):
        there = pl.ds(pl.multiple_of(((z + zr) % 4) * QUART, 128), QUART)
        rows = jnp.dot(gd[:, :, zr].reshape(ROWS, QUART), head[there], preferred_element_type=f32)
        acc[...] = rows if zr == 0 else acc[...] + rows
    for xr in range(4):
        for yr in range(4):
            to = ((x + xr) % 4) * 4 + (y + yr) % 4
            draft_ref[pl.ds(pl.multiple_of(to * 16, 16), 16)] = acc[pl.ds((xr * 4 + yr) * 16, 16)]
    draft_top, draft_sum = local_stats(draft_ref)

    lane = lax.broadcasted_iota(jnp.int32, (ROWS, 128), 1)
    packed = jnp.zeros((ROWS, 128), f32)
    for i, value in enumerate((main_top, main_sum, picked, draft_top, draft_sum)):
        packed = jnp.where(lane == i, value, packed)
    mine8 = packed.T[:8]

    def merge(tops, sums):
        top = jnp.max(tops, axis=0, keepdims=True)
        return top, jnp.sum(sums * jnp.exp(tops - top), axis=0, keepdims=True)

    for phase, axis in enumerate((2, 1, 0)):
        stats[phase, at[axis]] = mine8

        def st_copy(k, source):
            ref = stats.at[phase, source]
            return pltpu.make_async_remote_copy(
                src_ref=ref,
                dst_ref=ref,
                send_sem=st_s.at[phase * 3 + k - 1],
                recv_sem=st_r.at[phase * 3 + k - 1],
                device_id=device(along(at, axis, k), core),
                device_id_type=MESH,
            )

        waits.send([st_copy(k, at[axis]) for k in (1, 3, 2)])
        for k in (1, 3, 2):
            st_copy(k, (at[axis] + 4 - k) % 4).wait_recv()
        got = stats[phase]
        m_top, m_sum = merge(got[:, 0], got[:, 1])
        d_top, d_sum = merge(got[:, 3], got[:, 4])
        pick = jnp.sum(got[:, 2], axis=0, keepdims=True)
        mine8 = jnp.concatenate([m_top, m_sum, pick, d_top, d_sum, jnp.zeros((3, ROWS), f32)], axis=0)

    m_lse = m_top + jnp.log(m_sum)
    d_lse = d_top + jnp.log(d_sum)
    lse_ref[...] = jnp.concatenate([m_lse, d_lse, jnp.zeros((6, ROWS), f32)], axis=0)

    member = lax.broadcasted_iota(jnp.int32, (REQS, ROWS), 0) == request_ref[...]
    partial = jnp.sum(jnp.where(member, pick - m_lse, 0.0), axis=1, keepdims=True)
    score_buf[core] = jnp.broadcast_to(partial, (REQS, 128))

    def sc_copy(source):
        ref = score_buf.at[source]
        return pltpu.make_async_remote_copy(
            src_ref=ref,
            dst_ref=ref,
            send_sem=sc_s,
            recv_sem=sc_r,
            device_id=device(at, 1 - core),
            device_id_type=MESH,
        )

    waits.send([sc_copy(core)])
    sc_copy(1 - core).wait_recv()
    score_ref[...] = score_buf[0] + score_buf[1]
    waits.finish()


def per_device(
    hidden,
    next_embedding,
    final_gain,
    hidden_gain,
    embed_gain,
    draft_gain,
    head_weight,
    proj_embed,
    proj_hidden,
    token_ids,
    row_request,
):
    gains = jnp.stack([final_gain, hidden_gain, embed_gain, draft_gain]).astype(f32)
    gains = jnp.pad(gains, ((0, 4), (0, 128 - FEAT)))
    vmem = pl.BlockSpec(memory_space=pltpu.VMEM)
    hbm = pl.BlockSpec(memory_space=pltpu.HBM)
    main, draft, lse, score = pl.pallas_call(
        kernel,
        name="heads",
        out_shape=(
            jax.ShapeDtypeStruct((ROWS, VOC), f32),
            jax.ShapeDtypeStruct((ROWS, VOC), f32),
            jax.ShapeDtypeStruct((8, ROWS), f32),
            jax.ShapeDtypeStruct((REQS, 128), f32),
        ),
        in_specs=[hbm] * 2 + [vmem] + [hbm] * 5,
        out_specs=(vmem,) * 4,
        scratch_shapes=[
            pltpu.VMEM((FEAT, ROWS), bf16),
            pltpu.VMEM((1, ROWS), jnp.int32),
            pltpu.VMEM((1, ROWS), jnp.int32),
            pltpu.VMEM((D, VOC), bf16),
            pltpu.VMEM((4, 4, 4, 8, ROWS), f32),
            pltpu.VMEM((4, 4, 4, FEAT, ROWS), bf16),
            pltpu.VMEM((4, 4, 4, FEAT, ROWS), bf16),
            pltpu.VMEM((4, FEAT, 2 * ROWS), bf16),
            pltpu.VMEM((4, FEAT, 2 * ROWS), bf16),
            pltpu.VMEM((4, FEAT, HALF), bf16),
            pltpu.VMEM((4, FEAT, HALF), bf16),
            pltpu.VMEM((4, 4, 2, 2, 8, HALF), f32),
            pltpu.VMEM((2, 3, 4, 2, 8, HALF), f32),
            pltpu.VMEM((2, 4, 2, 8, HALF), f32),
            pltpu.VMEM((2, 8, 8, HALF), f32),
            pltpu.VMEM((4, 16, 128), f32),
            pltpu.VMEM((4, 4, 4, 16, QUART), bf16),
            pltpu.VMEM((ROWS, VOC), f32),
            pltpu.VMEM((3, 4, 8, ROWS), f32),
            pltpu.VMEM((2, REQS, 128), f32),
            DMA((4,)),
            DMA((6,)),
            DMA((9,)),
            DMA((9,)),
            DMA((2, 3)),
            DMA((2, 3)),
            DMA((2, 8)),
            DMA((2, 8)),
            DMA((63,)),
            DMA((63,)),
            DMA((6,)),
            DMA((6,)),
            DMA((16,)),
            DMA((16,)),
            DMA((3,)),
            DMA((3,)),
            DMA((63,)),
            DMA((63,)),
            DMA((9,)),
            DMA((9,)),
            DMA,
            DMA,
        ],
        compiler_params=pltpu.CompilerParams(
            collective_id=0, has_side_effects=True, vmem_limit_bytes=58 * 2**20
        ),
        cost_estimate=pl.CostEstimate(flops=8_300_000_000, bytes_accessed=20_000_000, transcendentals=600_000),
    )(
        hidden.T,
        next_embedding.T,
        gains,
        token_ids[None, :],
        row_request[None, :],
        head_weight,
        proj_embed,
        proj_hidden,
    )
    return (main - lse[0][:, None], draft - lse[1][:, None], score[:, 0])


def solution(mesh):
    return jax.shard_map(
        per_device,
        mesh=mesh,
        in_specs=(
            P("req", "vocab"),
            P("req", "vocab"),
            P("vocab"),
            P("vocab"),
            P("vocab"),
            P("vocab"),
            P(None, "vocab"),
            P("vocab", None),
            P("vocab", None),
            P("req"),
            P("req"),
        ),
        out_specs=(P("req", "vocab"), P("req", "vocab"), P()),
        check_vma=False,
    )
```

time: 1230 us -> 111 us (0.09)
  blocking collectives: 762 us -> 0 us
  waiting for transfers between devices: 411 us -> 0 us
  Pallas kernels: 0 us -> 102 us
  matrix products: 26.5 us -> 0 us
  between operations: 13.8 us -> 0.64 us
    psum x4 -> x0, blocking collectives: 587 us -> none  [the longest x1 180 us: per_device(): lax.psum((jnp.sum(hidden_wide * hidden_wide, axis=1), jnp.sum(embed_wide...]
    reduce_scatter x1 -> x0, waiting for transfers between devices: 357 us -> none  [per_device(): lax.psum_scatter(lax.dot_general(proj_embed, normed_embed, contract_cross...]
    pmax x1 -> x0, blocking collectives: 175 us -> none  [per_device(): main_peak = lax.pmax(main_local, 'vocab')]
    pallas_call x0 -> x1, Pallas kernels: none -> 102 us  [per_device(): pl.pallas_call(kernel, name='heads', out_shape=(jax.ShapeDtypeStruct((ROW...]
    all_gather x2 -> x0, waiting for transfers between devices: 54.4 us -> none  [the longest x1 54.3 us: per_device(): lax.all_gather(normed_draft, 'vocab', axis=0, tiled=True)]
    dot_general x5 -> x0, matrix products: 26.5 us -> none  [the longest x1 11.2 us: per_device(): lax.dot_general(lax.all_gather(normed_draft, 'vocab', axis=0, tiled=True)...]
  transfers between devices with their start and end apart: 3 -> 0, of which waited for: 2 -> 0; matrix products, arithmetic and copies ran while one was open for 1% -> 0% of each run, Pallas kernels for 0% -> 0%
where the time goes in v2:
time: 111 us; the launch traced here: 110 us
  Pallas kernels  102 us (92%)
  other arithmetic  4.37 us (4%)
  local copies, waits for them, and re-layouts  2.16 us (2%)
    pallas_call x1, Pallas kernels, per_device(): pl.pallas_call(kernel, name='heads', out_shape=(jax.ShapeDtypeStruct((ROW...  102 us
    sub x1, other arithmetic, per_device(): return (main - lse[0][:, None], draft - lse[1][:, None], score[:, 0])  3.06 us

profile of v2, /device:TPU:0, one launch (start us, length us, event | category | flops | bytes accessed | tf_op | source)
XLA Modules:
  0.0 109.6 jit_solution(707774979951775761)
XLA Ops:
  0.6 1.3 %fusion.9.gains_ref = f32[8,128]{1,0:T(8,128)} fusion(bf16[1,112]{1,0:T(2,128)(2,1)} %bitcast.12, bf16[1,112]{1,0:T(2,128)(2,1)} %bitcast.13, bf16[1,112]{1,0:T(2,128)(2,1)} %bitcast.14, bf16[1,112]{1,0:T(2,128)(2,1)} %bitcast.15), kind=kLoop, calls=%fused_computation.14 | loop fusion | flops 19456 | bytes 4992 | tf_op jit(solution)/shard_map/jit(_pad)/pad | solution.py:539
  1.9 102.4 %heads.1 = (f32[256,1024]{1,0:T(8,128)}, f32[256,1024]{1,0:T(8,128)}, f32[8,256]{1,0:T(8,128)}, f32[64,128]{1,0:T(8,128)}) custom-call(bf16[112,256]{1,0:T(8,128)(2,1)} %bitcast.16, bf16[112,256]{1,0:T(8,128)(2,1)} %bitcast.17, f32[8,128]{1,0:T(8,128)} %fusion.9.gains_ref, s32[1,256]{1,0:T(1,128)} %bitcast.18, s32[1,256]{1,0:T(1,128)} %bitcast.19, ...), custom_call_target="tpu_custom_call" | custom-call | flops 8300000256 | bytes 20000000 | tf_op jit(solution)/shard_map/heads/pallas_call | solution.py:542
  104.4 1.4 %slice_reduce_fusion = f32[64]{0:T(128)} fusion(f32[64,128]{1,0:T(8,128)} %get-tuple-element.10), kind=kLoop, calls=%fused_computation.2 | loop fusion | bytes 512 | tf_op jit(solution)/shard_map/slice | solution.py:611
  105.8 0.8 fusion.13
  106.5 3.1 %broadcast_subtract_fusion = (f32[256,1024]{1,0:T(8,128)}, f32[256,1024]{1,0:T(8,128)}) fusion(f32[256,1024]{1,0:T(8,128)} %get-tuple-element.9, f32[256]{0:T(256)S(1)} %bitcast.10, f32[256,1024]{1,0:T(8,128)} %get-tuple-element.7, f32[256]{0:T(256)S(1)} %bitcast.11), kind=kLoop, calls=%fused_computation | loop fusion | flops 524288 | bytes 4196352 | tf_op jit(solution)/shard_map/sub | solution.py:611

commit v3 on v2

v3 whole, which is shorter than its diff:
```python
import jax
import jax.numpy as jnp
from jax import lax
from jax.experimental import pallas as pl
from jax.experimental.pallas import tpu as pltpu
from jax.sharding import PartitionSpec as P

D = 7168
REQS = 64
SIDE = 4
FEAT = 112
ROWS = 256
VOC = 1024
QUART = D // SIDE
HALF = QUART // 2

epsilon = 1e-06
MESH = pl.DeviceIdType.MESH
DMA = pltpu.SemaphoreType.DMA
f32 = jnp.float32
bf16 = jnp.bfloat16
FIRST = (((0,), (0,)), ((), ()))

H_ORDERS = ((2, 0, 1), (2, 1, 0), (0, 1, 2))
G_ORDERS = ((2, 1, 0), (0, 2, 1), (1, 0, 2))
H_EARLY = 64
H_PARTS = ((0, 64, 0, 128), (0, 64, 128, 128), (64, 48, 0, 256))
G_PARTS = ((0, 640), (640, 640), (1280, 512))

PIECES = ((0, 512), (512, 384))

OTHERS, ALL = pl.ds(1, 3), pl.ds(0, 4)
STEPS = {
    "0a": (0, (0, 0, 0)),
    "0b": (1, (0, 0, 0)),
    "1b": (1, (OTHERS, 0, 0)),
    "Lb": (1, (ALL, 0, 0)),
    "Lc": (2, (ALL, 0, 0)),
    "Pc": (2, (ALL, OTHERS, 0)),
    "Sc": (2, (ALL, ALL, 0)),
}


def coords():
    v = lax.axis_index("vocab")
    return (v // 16, (v // 4) % 4, v % 4)


def device(at, core):
    return (core, (at[0] * 4 + at[1]) * 4 + at[2])


def along(at, axis, step):
    moved = list(at)
    moved[axis] = (at[axis] + step) % 4
    return tuple(moved)


class Gather:
    def __init__(self, waits, name, view, order, send, recv, base):
        self.waits, self.name, self.view, self.order = waits, name, view, order
        self.sems, self.base = (send, recv), base

    def copy(self, step, k, landed):
        place, blocks = STEPS[step]
        there = list(blocks)
        there[place] = 4 - k
        index = self.base + list(STEPS).index(step) * 3 + k - 1
        src, dst = (self.view(tuple(b[self.order.index(a)] for a in range(3))) for b in (blocks, there))
        return pltpu.make_async_remote_copy(
            src_ref=dst if landed else src,
            dst_ref=dst,
            send_sem=self.sems[0].at[index],
            recv_sem=self.sems[1].at[index],
            device_id=device(along(coords(), self.order[place], k), lax.axis_index("req")),
            device_id_type=MESH,
        )

    def start(self, *steps):
        for step in steps:
            self.waits.send([self.copy(step, k, False) for k in (1, 3, 2)])

            def wait(step=step):
                for k in (1, 3, 2):
                    self.copy(step, k, True).wait_recv()

            self.waits.expect(self.name + step, wait)

    def wait(self, *steps):
        for step in steps:
            self.waits.receive(self.name + step)


def turn(row):
    return jnp.broadcast_to(row, (128, row.shape[1])).T


class Waits:
    def __init__(self):
        self.receives, self.sends = {}, []

    def send(self, copies):
        for copy in copies:
            copy.start()
        self.sends += copies

    def expect(self, name, wait):
        self.receives[name] = wait

    def receive(self, name):
        self.receives.pop(name)()

    def finish(self):
        for name in list(self.receives):
            self.receive(name)
        for copy in self.sends:
            copy.wait_send()


def kernel(
    hid_hbm, emb_hbm, rows_ref, token_hbm, request_hbm, head_ref, pe_ref, ph_ref,
    main_hbm, draft_hbm, main_lse_ref, draft_lse_ref, score_ref,
    main_ref, draft_ref, token_ref, request_ref, head, small, gath, normed, xraw, xsq, xe, xh, we, wh, part, got1, sum1, got2, sq, gd, acc, stats, score_buf,
    head_sem, own_sem,
    small_s, small_r, w_s, w_r, x_s, x_r, h_s, h_r, r1_s, r1_r, r2_s, r2_r, q_s, q_r, g_s, g_r,
    st_s, st_r, sc_s, sc_r,
):
    core = lax.axis_index("req")
    at = coords()
    x, y, z = at
    waits = Waits()
    mine = pl.ds(pl.multiple_of(core * ROWS, 128), ROWS)

    def columns(zz):
        return pl.ds(pl.multiple_of(zz * QUART + core * HALF, 128), HALF)

    row_copies = [
        pltpu.make_async_copy(hid_hbm, xraw.at[z, 1, :, mine], own_sem.at[2]),
        pltpu.make_async_copy(emb_hbm, xraw.at[z, 0, :, mine], own_sem.at[3]),
        pltpu.make_async_copy(hid_hbm, gath.at[0, 0, 0], own_sem.at[4]),
    ]
    own_copies = [
        pltpu.make_async_copy(token_hbm, token_ref, own_sem.at[5]),
        pltpu.make_async_copy(request_hbm, request_ref, own_sem.at[6]),
        pltpu.make_async_copy(pe_ref.at[:, columns(z)], we.at[z], own_sem.at[0]),
        pltpu.make_async_copy(ph_ref.at[:, columns(z)], wh.at[z], own_sem.at[1]),
    ]
    head_copies = [
        pltpu.make_async_copy(
            head_ref.at[pl.ds(i * QUART, QUART)], head.at[pl.ds(i * QUART, QUART)], head_sem.at[i]
        )
        for i in range(4)
    ]
    for copy in row_copies:
        copy.start()

    barrier = pltpu.get_barrier_semaphore()
    partners = [device(at, 1 - core)] + [
        device(along(at, axis, k), c) for axis in (2, 1, 0) for k in (1, 2, 3) for c in (0, 1)
    ]
    for partner in partners:
        pl.semaphore_signal(barrier, inc=1, device_id=partner, device_id_type=MESH)
    for copy in own_copies + head_copies:
        copy.start()

    for copy in row_copies:
        copy.wait()
    emb = xraw[z, 0, :, mine].astype(f32)
    hid = xraw[z, 1, :, mine].astype(f32)
    small[0, 0, 0] = jnp.concatenate(
        [
            jnp.sum(emb * emb, axis=0, keepdims=True),
            jnp.sum(hid * hid, axis=0, keepdims=True),
            rows_ref[0:4],
            jnp.zeros((2, ROWS), f32),
        ],
        axis=0,
    )
    pl.semaphore_wait(barrier, len(partners))

    def small_copy(phase, k, landed):
        blocks = [(0, 0, 0), (0, 0, pl.ds(0, 4)), (0, pl.ds(0, 4), pl.ds(0, 4))][phase]
        there = list(blocks)
        there[2 - phase] = 4 - k
        return pltpu.make_async_remote_copy(
            src_ref=small.at[tuple(there) if landed else blocks],
            dst_ref=small.at[tuple(there)],
            send_sem=small_s.at[phase * 3 + k - 1],
            recv_sem=small_r.at[phase * 3 + k - 1],
            device_id=device(along(at, 2 - phase, k), core),
            device_id_type=MESH,
        )

    def small_start(phase):
        waits.send([small_copy(phase, k, False) for k in (1, 3, 2)])

    def small_wait(phase):
        for k in (1, 3, 2):
            small_copy(phase, k, True).wait_recv()

    def x_copy(k, forward):
        to = ((core + 1) % 2) if forward or k == 0 else core
        ref = xraw.at[(z + 4 - k) % 4 if forward else z, :, :, mine]
        index = k + 3 if forward else k
        return pltpu.make_async_remote_copy(
            src_ref=ref,
            dst_ref=ref,
            send_sem=x_s.at[index],
            recv_sem=x_r.at[index],
            device_id=device(at if forward else along(at, 2, k), to),
            device_id_type=MESH,
        )

    def x_wait(k, forward):
        other = pl.ds(pl.multiple_of((1 - core) * ROWS, 128), ROWS)
        ref = xraw.at[(z + 4 - k) % 4, :, :, other if forward or k == 0 else mine]
        index = k + 3 if forward else k
        pltpu.make_async_remote_copy(
            src_ref=ref,
            dst_ref=ref,
            send_sem=x_s.at[index],
            recv_sem=x_r.at[index],
            device_id=device(at, 1 - core),
            device_id_type=MESH,
        ).wait_recv()

    def x_arrive():
        for k in (1, 3, 2):
            x_wait(k, False)
            waits.send([x_copy(k, True)])

    def x_all():
        for k in (1, 3, 2):
            x_wait(k, True)
        x_wait(0, False)

    small_start(0)
    waits.send([x_copy(k, False) for k in (1, 3, 2, 0)])
    waits.expect("x", x_arrive)
    waits.expect("x forwarded", x_all)

    ha, hb, hc = [
        Gather(
            waits,
            "h%d" % p,
            lambda s, r=r, n=n, c=c, m=m: gath.at[s + (pl.ds(r, n), pl.ds(c, m))],
            order,
            h_s,
            h_r,
            21 * p,
        )
        for p, (order, (r, n, c, m)) in enumerate(zip(H_ORDERS, H_PARTS))
    ]
    w_pairs = ((pe_ref, we), (ph_ref, wh))

    def w_copy(k, j, p, src, dst):
        return pltpu.make_async_remote_copy(
            src_ref=src,
            dst_ref=dst,
            send_sem=w_s.at[j, p * 3 + k - 1],
            recv_sem=w_r.at[j, p * 3 + k - 1],
            device_id=device(along(at, 2, k), core),
            device_id_type=MESH,
        )

    def w_start(p):
        c, n = PIECES[p]
        for k in (1, 3, 2):
            there = pl.ds(pl.multiple_of((z + k) % 4 * QUART + core * HALF + c, 128), n)
            waits.send(
                [
                    w_copy(k, j, p, src.at[:, there], dst.at[z, :, pl.ds(c, n)])
                    for j, (src, dst) in enumerate(w_pairs)
                ]
            )

        def w_wait(ks):
            for k in ks:
                for j, (_, dst) in enumerate(w_pairs):
                    ref = dst.at[(z + 4 - k) % 4, :, pl.ds(c, n)]
                    w_copy(k, j, p, ref, ref).wait_recv()

        waits.expect("w%dnear" % p, lambda: w_wait((1, 3)))
        waits.expect("w%d" % p, lambda: w_wait((2,)))

    small_wait(0)
    small_start(1)
    hc.start("0a", "0b")
    waits.receive("x")
    w_start(0)
    w_start(1)
    small_wait(1)
    small_start(2)
    for zr in (1, 2, 3):
        gath[0, 0, zr, :H_EARLY] = xraw[(z + zr) % 4, 1, :H_EARLY, mine]
    ha.start("Lb")
    hb.start("Lb")
    hc.wait("0a")
    hc.start("1b")
    ha.start("Lc")
    hb.start("Lc")
    small_wait(2)

    xsq[core] = jnp.sum(small[...].reshape(64, 8, ROWS), axis=0)

    def xsq_copy(which):
        ref = xsq.at[which]
        return pltpu.make_async_remote_copy(
            src_ref=ref,
            dst_ref=ref,
            send_sem=x_s.at[7],
            recv_sem=x_r.at[7],
            device_id=device(at, 1 - core),
            device_id_type=MESH,
        )

    waits.send([xsq_copy(core)])
    waits.expect("xsq", xsq_copy(1 - core).wait_recv)

    ha.wait("Lb")
    ha.start("Pc")
    hb.wait("Lb")
    hb.start("Pc")

    waits.receive("x forwarded")
    waits.receive("xsq")
    hid_scale = lax.rsqrt(xsq[core, 1:2] / D + epsilon)
    scales = [
        lax.rsqrt(jnp.concatenate([xsq[0, j : j + 1], xsq[1, j : j + 1]], axis=1) / D + epsilon) for j in (0, 1)
    ]
    for zr in range(4):
        block_gains = small[0, 0, zr, :, :128].T
        there = (z + zr) % 4
        for j, buf in enumerate((xe, xh)):
            raw = xraw[there, j].astype(f32)
            buf[there] = (raw * scales[j] * block_gains[:FEAT, 5 - j : 6 - j]).astype(bf16)
    for copy in own_copies:
        copy.wait()
    draft_gain = jnp.concatenate(
        [
            small[(z + 4 - x) % 4, (yy + 4 - y) % 4, (zz + 4 - z) % 4, 2:3, :FEAT]
            for yy in range(4)
            for zz in range(4)
        ],
        axis=1,
    )
    token = turn(token_ref[...].astype(f32))
    base = (lax.axis_index("vocab") * VOC).astype(f32)

    line = [(k, dc) for k in range(4) for dc in (0, 1)][1:]

    def r1_copy(p, half, k):
        lanes = pl.ds(*PIECES[p])
        to = (at[half] + k) % 4
        src = part.at[to, :, :, 0, :, lanes] if half == 0 else part.at[:, to, :, 1, :, lanes]
        return pltpu.make_async_remote_copy(
            src_ref=src,
            dst_ref=got1.at[half, k - 1, :, :, :, lanes],
            send_sem=r1_s.at[p * 6 + half * 3 + k - 1],
            recv_sem=r1_r.at[p * 6 + half * 3 + k - 1],
            device_id=device(along(at, half, k), core),
            device_id_type=MESH,
        )

    def r2_copy(p, half, k, dc):
        lanes = pl.ds(*PIECES[p])
        to = (core + dc) % 2
        axis = 1 - half
        return pltpu.make_async_remote_copy(
            src_ref=sum1.at[half, (at[axis] + k) % 4, to, :, lanes],
            dst_ref=got2.at[half, k * 2 + dc, :, lanes],
            send_sem=r2_s.at[p * 16 + half * 8 + k * 2 + dc],
            recv_sem=r2_r.at[p * 16 + half * 8 + k * 2 + dc],
            device_id=device(along(at, axis, k), to),
            device_id_type=MESH,
        )

    for p, (c0, n) in enumerate(PIECES):
        lanes = pl.ds(c0, n)
        waits.receive("w%dnear" % p)
        waits.receive("w%d" % p)
        for c in (0, 1):
            reqs = pl.ds(c * ROWS, ROWS)
            rows = lax.dot_general(
                xe[:, :, reqs].reshape(4 * FEAT, ROWS), we[:, :, lanes].reshape(4 * FEAT, n), FIRST,
                preferred_element_type=f32,
            ) + lax.dot_general(
                xh[:, :, reqs].reshape(4 * FEAT, ROWS), wh[:, :, lanes].reshape(4 * FEAT, n), FIRST,
                preferred_element_type=f32,
            )
            part[:, :, c, :, :, lanes] = rows.reshape(4, 4, 2, 8, n)
        for half in (0, 1):
            for k in (1, 3, 2):
                waits.send([r1_copy(p, half, k)])
                waits.expect("r1%d%d%d" % (p, half, k), r1_copy(p, half, k).wait_recv)
    hc.wait("0b", "1b")
    hc.start("Sc")
    for p, (c0, n) in enumerate(PIECES):
        lanes = pl.ds(c0, n)
        for half in (0, 1):
            own = part[x, :, :, 0, :, lanes] if half == 0 else part[:, y, :, 1, :, lanes]
            for k in (1, 3, 2):
                waits.receive("r1%d%d%d" % (p, half, k))
                own = own + got1[half, k - 1, :, :, :, lanes]
            sum1[half, :, :, :, lanes] = own
            for k, dc in line:
                waits.send([r2_copy(p, half, k, dc)])
                waits.expect("r2%d%d%d%d" % (p, half, k, dc), r2_copy(p, half, k, dc).wait_recv)

    state_halves = []
    for half in (0, 1):
        for p in (0, 1):
            for k, dc in line:
                waits.receive("r2%d%d%d%d" % (p, half, k, dc))
        same = sum1[half, at[1 - half], core]
        for k in (1, 2, 3):
            same = same + got2[half, k * 2]
        other = got2[half, 1] + got2[half, 3] + got2[half, 5] + got2[half, 7]
        state_halves.append(
            jnp.concatenate(
                [jnp.where(core == 0, same, other), jnp.where(core == 0, other, same)], axis=1
            )
        )
    state = jnp.concatenate(state_halves, axis=0)
    sq[z] = jnp.broadcast_to(jnp.sum(state * state, axis=1, keepdims=True), (16, 128))

    def q_copy(k, source):
        ref = sq.at[source]
        return pltpu.make_async_remote_copy(
            src_ref=ref,
            dst_ref=ref,
            send_sem=q_s.at[k - 1],
            recv_sem=q_r.at[k - 1],
            device_id=device(along(at, 2, k), core),
            device_id_type=MESH,
        )

    waits.send([q_copy(k, z) for k in (1, 3, 2)])
    for k in (1, 3, 2):
        waits.expect("q%d" % k, q_copy(k, (z + 4 - k) % 4).wait_recv)
    ha.wait("Lc", "Pc")
    hb.wait("Lc", "Pc")
    hc.wait("Sc")

    def norm(xr, _):
        gain = small[xr].reshape(16, 8, ROWS)[:, 3, :128].T
        for yr in range(4):
            for zr in range(4):
                block = gath[xr, yr, zr].astype(f32) * hid_scale * gain[:FEAT, yr * 4 + zr : yr * 4 + zr + 1]
                normed[(x + xr) % 4, (y + yr) % 4, (z + zr) % 4] = block.astype(bf16)
        return 0

    lax.fori_loop(0, 4, norm, 0)
    for copy in head_copies:
        copy.wait()
    for k in (1, 3, 2):
        waits.receive("q%d" % k)
    total = jnp.sum(sq[...], axis=0)[:, :1]
    gd[0, 0, 0] = (state * lax.rsqrt(total / D + epsilon) * draft_gain).astype(bf16)

    earlier = list(waits.sends)
    gs = [
        Gather(waits, "g%d" % p, lambda s, c=c, n=n: gd.at[s + (slice(None), pl.ds(c, n))], order, g_s, g_r, 21 * p)
        for p, (order, (c, n)) in enumerate(zip(G_ORDERS, G_PARTS))
    ]
    for g in gs:
        g.start("0a")
    def main_dot(q):
        rows = lax.dot_general(
            normed[q].reshape(QUART, ROWS), head[pl.ds(q * QUART, QUART)], FIRST, preferred_element_type=f32
        )
        main_ref[...] = rows if q == 0 else main_ref[...] + rows

    for g in gs:
        g.wait("0a")
        g.start("Lb")
    for g in gs:
        g.start("Lc")
    main_dot(0)
    for g in gs:
        g.wait("Lb")
        g.start("Pc")
    main_dot(1)
    main_dot(2)
    main_dot(3)

    def local_stats(ref):
        logits = ref[...]
        top = jnp.max(logits, axis=1, keepdims=True)
        return top, jnp.sum(jnp.exp(logits - top), axis=1, keepdims=True)

    main_out = pltpu.make_async_copy(main_ref, main_hbm, own_sem.at[7])
    main_out.start()
    main_top, main_sum = local_stats(main_ref)
    column = lax.broadcasted_iota(jnp.int32, (ROWS, VOC), 1).astype(f32) + base
    picked = jnp.sum(jnp.where(column == token[:, :1], main_ref[...], 0.0), axis=1, keepdims=True)

    def pack(values):
        lane = lax.broadcasted_iota(jnp.int32, (ROWS, 128), 1)
        packed = jnp.zeros((ROWS, 128), f32)
        for i, value in enumerate(values):
            packed = jnp.where(lane == i, value, packed)
        return packed.T[:8]

    def st_copy(which, phase, k, source):
        ref = stats.at[which, phase, source]
        index = which * 9 + phase * 3 + k - 1
        return pltpu.make_async_remote_copy(
            src_ref=ref,
            dst_ref=ref,
            send_sem=st_s.at[index],
            recv_sem=st_r.at[index],
            device_id=device(along(at, 2 - phase, k), core),
            device_id_type=MESH,
        )

    def st_start(which, phase, block):
        here = at[2 - phase]
        stats[which, phase, here] = block
        waits.send([st_copy(which, phase, k, here) for k in (1, 3, 2)])
        for k in (1, 3, 2):
            source = (here + 4 - k) % 4
            waits.expect("st%d%d%d" % (which, phase, k), st_copy(which, phase, k, source).wait_recv)

    def st_finish(which, phase):
        for k in (1, 3, 2):
            waits.receive("st%d%d%d" % (which, phase, k))
        got = stats[which, phase]
        tops = got[:, 0]
        top = jnp.max(tops, axis=0, keepdims=True)
        total = jnp.sum(got[:, 1] * jnp.exp(tops - top), axis=0, keepdims=True)
        pick = jnp.sum(got[:, 2], axis=0, keepdims=True)
        return jnp.concatenate([top, total, pick, jnp.zeros((5, ROWS), f32)], axis=0)

    st_start(0, 0, pack((main_top, main_sum, picked)))
    for copy in earlier:
        copy.wait_send()
    waits.sends = waits.sends[len(earlier) :]

    for g in gs:
        g.wait("Lc", "Pc")

    def draft_dot(zr):
        there = pl.ds(pl.multiple_of(((z + zr) % 4) * QUART, 128), QUART)
        rows = jnp.dot(gd[:, :, zr].reshape(ROWS, QUART), head[there], preferred_element_type=f32)
        acc[...] = rows if zr == 0 else acc[...] + rows

    draft_dot(0)
    draft_dot(1)
    st_start(0, 1, st_finish(0, 0))
    draft_dot(2)
    draft_dot(3)
    for xr in range(4):
        for yr in range(4):
            to = ((x + xr) % 4) * 4 + (y + yr) % 4
            draft_ref[pl.ds(pl.multiple_of(to * 16, 16), 16)] = acc[pl.ds((xr * 4 + yr) * 16, 16)]
    draft_out = pltpu.make_async_copy(draft_ref, draft_hbm, own_sem.at[8])
    draft_out.start()
    draft_top, draft_sum = local_stats(draft_ref)
    st_start(1, 0, pack((draft_top, draft_sum)))
    st_start(0, 2, st_finish(0, 1))
    st_start(1, 1, st_finish(1, 0))
    main_all = st_finish(0, 2)
    main_lse = main_all[0:1] + jnp.log(main_all[1:2])
    main_lse_ref[...] = main_lse

    member = lax.broadcasted_iota(jnp.int32, (REQS, ROWS), 0) == request_ref[...]
    partial = jnp.sum(jnp.where(member, main_all[2:3] - main_lse, 0.0), axis=1, keepdims=True)
    score_buf[core] = jnp.broadcast_to(partial, (REQS, 128))

    def sc_copy(source):
        ref = score_buf.at[source]
        return pltpu.make_async_remote_copy(
            src_ref=ref,
            dst_ref=ref,
            send_sem=sc_s,
            recv_sem=sc_r,
            device_id=device(at, 1 - core),
            device_id_type=MESH,
        )

    waits.send([sc_copy(core)])
    st_start(1, 2, st_finish(1, 1))
    sc_copy(1 - core).wait_recv()
    score_ref[...] = (score_buf[0] + score_buf[1]).T[:1]
    draft_all = st_finish(1, 2)
    draft_lse_ref[...] = draft_all[0:1] + jnp.log(draft_all[1:2])
    main_out.wait()
    draft_out.wait()
    waits.finish()


def per_device(
    hidden,
    next_embedding,
    final_gain,
    hidden_gain,
    embed_gain,
    draft_gain,
    head_weight,
    proj_embed,
    proj_hidden,
    token_ids,
    row_request,
):
    rows = jnp.stack([draft_gain, final_gain, hidden_gain, embed_gain]).astype(f32)
    rows = jnp.pad(rows, ((0, 4), (0, ROWS - FEAT)))
    vmem = pl.BlockSpec(memory_space=pltpu.VMEM)
    hbm = pl.BlockSpec(memory_space=pltpu.HBM)
    main, draft, main_lse, draft_lse, score = pl.pallas_call(
        kernel,
        name="heads",
        out_shape=(
            jax.ShapeDtypeStruct((ROWS, VOC), f32),
            jax.ShapeDtypeStruct((ROWS, VOC), f32),
            jax.ShapeDtypeStruct((1, ROWS), f32),
            jax.ShapeDtypeStruct((1, ROWS), f32),
            jax.ShapeDtypeStruct((1, REQS), f32),
        ),
        in_specs=[hbm] * 2 + [vmem] + [hbm] * 5,
        out_specs=(hbm,) * 2 + (vmem,) * 3,
        scratch_shapes=[
            pltpu.VMEM((ROWS, VOC), f32),
            pltpu.VMEM((ROWS, VOC), f32),
            pltpu.VMEM((1, ROWS), jnp.int32),
            pltpu.VMEM((1, ROWS), jnp.int32),
            pltpu.VMEM((D, VOC), bf16),
            pltpu.VMEM((4, 4, 4, 8, ROWS), f32),
            pltpu.VMEM((4, 4, 4, FEAT, ROWS), bf16),
            pltpu.VMEM((4, 4, 4, FEAT, ROWS), bf16),
            pltpu.VMEM((4, 2, FEAT, 2 * ROWS), bf16),
            pltpu.VMEM((2, 8, ROWS), f32),
            pltpu.VMEM((4, FEAT, 2 * ROWS), bf16),
            pltpu.VMEM((4, FEAT, 2 * ROWS), bf16),
            pltpu.VMEM((4, FEAT, HALF), bf16),
            pltpu.VMEM((4, FEAT, HALF), bf16),
            pltpu.VMEM((4, 4, 2, 2, 8, HALF), f32),
            pltpu.VMEM((2, 3, 4, 2, 8, HALF), f32),
            pltpu.VMEM((2, 4, 2, 8, HALF), f32),
            pltpu.VMEM((2, 8, 8, HALF), f32),
            pltpu.VMEM((4, 16, 128), f32),
            pltpu.VMEM((4, 4, 4, 16, QUART), bf16),
            pltpu.VMEM((ROWS, VOC), f32),
            pltpu.VMEM((2, 3, 4, 8, ROWS), f32),
            pltpu.VMEM((2, REQS, 128), f32),
            DMA((4,)),
            DMA((9,)),
            DMA((9,)),
            DMA((9,)),
            DMA((2, 6)),
            DMA((2, 6)),
            DMA((8,)),
            DMA((8,)),
            DMA((63,)),
            DMA((63,)),
            DMA((12,)),
            DMA((12,)),
            DMA((32,)),
            DMA((32,)),
            DMA((3,)),
            DMA((3,)),
            DMA((63,)),
            DMA((63,)),
            DMA((18,)),
            DMA((18,)),
            DMA,
            DMA,
        ],
        compiler_params=pltpu.CompilerParams(
            collective_id=0, has_side_effects=True, vmem_limit_bytes=58 * 2**20
        ),
        cost_estimate=pl.CostEstimate(flops=8_300_000_000, bytes_accessed=20_000_000, transcendentals=600_000),
    )(
        hidden.T,
        next_embedding.T,
        rows,
        token_ids[None, :],
        row_request[None, :],
        head_weight,
        proj_embed,
        proj_hidden,
    )
    return (main - main_lse[0][:, None], draft - draft_lse[0][:, None], score[0])


def solution(mesh):
    return jax.shard_map(
        per_device,
        mesh=mesh,
        in_specs=(
            P("req", "vocab"),
            P("req", "vocab"),
            P("vocab"),
            P("vocab"),
            P("vocab"),
            P("vocab"),
            P(None, "vocab"),
            P("vocab", None),
            P("vocab", None),
            P("req"),
            P("req"),
        ),
        out_specs=(P("req", "vocab"), P("req", "vocab"), P()),
        check_vma=False,
    )
```

time: 111 us -> 104 us (0.937)
  Pallas kernels: 102 us -> 97.8 us
  local copies, waits for them, and re-layouts: 2.16 us -> 0.52 us
    pallas_call x1, Pallas kernels: 102 us -> 97.8 us  [per_device(): pl.pallas_call(kernel, name='heads', out_shape=(jax.ShapeDtypeStruct((ROW...]
    slice x2 -> x0, local copies, waits for them, and re-layouts: 2.16 us -> none  [per_device(): return (main - lse[0][:, None], draft - lse[1][:, None], score[:, 0])]
where the time goes in v3:
time: 104 us; the launch traced here: 103 us
  Pallas kernels  97.8 us (94%)
  other arithmetic  4.38 us (4%)
    pallas_call x1, Pallas kernels, per_device(): pl.pallas_call(kernel, name='heads', out_shape=(jax.ShapeDtypeStruct((ROW...  97.8 us
    sub x1, other arithmetic, per_device(): draft - draft_lse[0][:, None]  3.07 us

profile of v3, /device:TPU:0, one launch (start us, length us, event | category | flops | bytes accessed | tf_op | source)
XLA Modules:
  0.0 103.4 jit_solution(12299211557748352357)
XLA Ops:
  0.6 1.3 %fusion.9.rows_ref = f32[8,256]{1,0:T(8,128)} fusion(bf16[1,112]{1,0:T(2,128)(2,1)} %bitcast.13, bf16[1,112]{1,0:T(2,128)(2,1)} %bitcast.14, bf16[1,112]{1,0:T(2,128)(2,1)} %bitcast.15, bf16[1,112]{1,0:T(2,128)(2,1)} %bitcast.16), kind=kLoop, calls=%fused_computation.13 | loop fusion | flops 38912 | bytes 9088 | tf_op jit(solution)/shard_map/jit(_pad)/pad | solution.py:607
  1.9 97.8 %heads.1 = (f32[256,1024]{1,0:T(8,128)}, f32[256,1024]{1,0:T(8,128)}, f32[1,256]{1,0:T(1,128)}, f32[1,256]{1,0:T(1,128)}, f32[1,64]{1,0:T(1,128)}) custom-call(bf16[112,256]{1,0:T(8,128)(2,1)} %bitcast.17, bf16[112,256]{1,0:T(8,128)(2,1)} %bitcast.18, f32[8,256]{1,0:T(8,128)} %fusion.9.rows_ref, s32[1,256]{1,0:T(1,128)} %bitcast.19, s32[1,256]{1,0:T(1,128)} %bitcast.20, ...), custom_call_target="tpu_custom_call" | custom-call | flops 8300000256 | bytes 20000000 | tf_op jit(solution)/shard_map/heads/pallas_call | solution.py:610
  99.8 0.0 copy-start
  99.8 3.1 %broadcast_subtract_fusion = (f32[256,1024]{1,0:T(8,128)}, f32[256,1024]{1,0:T(8,128)}) fusion(f32[256,1024]{1,0:T(8,128)} %get-tuple-element.10, f32[256]{0:T(256)} %bitcast.12, f32[256,1024]{1,0:T(8,128)} %get-tuple-element.8, f32[256]{0:T(256)} %bitcast.11), kind=kLoop, calls=%fused_computation | loop fusion | flops 524288 | bytes 4196352 | tf_op jit(solution)/shard_map/sub | solution.py:683
  102.8 0.0 copy-done
  102.8 0.5 copy.15
Async XLA Ops:
  99.8 3.1 %copy-start = (f32[1,64]{1,0:T(1,128)S(1)}, f32[1,64]{1,0:T(1,128)}, u32[]{:S(2)}) copy-start(f32[1,64]{1,0:T(1,128)} %get-tuple-element.12) | copy-start | bytes 772

commit v4 on v3

--- a/solution.py
+++ b/solution.py
@@ -118,9 +118,9 @@
 
 
 def kernel(
-    hid_hbm, emb_hbm, rows_ref, token_hbm, request_hbm, head_ref, pe_ref, ph_ref,
+    hid_hbm, emb_hbm, gain_a, gain_b, gain_c, gain_d, token_hbm, request_hbm, head_ref, pe_ref, ph_ref,
     main_hbm, draft_hbm, main_lse_ref, draft_lse_ref, score_ref,
-    main_ref, draft_ref, token_ref, request_ref, head, small, gath, normed, xraw, xsq, xe, xh, we, wh, part, got1, sum1, got2, sq, gd, acc, stats, score_buf,
+    main_ref, draft_ref, near_a, near_b, near_c, near_d, token_ref, request_ref, head, small, gath, normed, xraw, xsq, xe, xh, we, wh, part, got1, sum1, got2, sq, gd, acc, stats, score_buf,
     head_sem, own_sem,
     small_s, small_r, w_s, w_r, x_s, x_r, h_s, h_r, r1_s, r1_r, r2_s, r2_r, q_s, q_r, g_s, g_r,
     st_s, st_r, sc_s, sc_r,
@@ -151,6 +151,11 @@
         )
         for i in range(4)
     ]
+    gains = (near_a, near_b, near_c, near_d)
+    row_copies += [
+        pltpu.make_async_copy(src, dst, own_sem.at[9 + j])
+        for j, (src, dst) in enumerate(zip((gain_a, gain_b, gain_c, gain_d), gains))
+    ]
     for copy in row_copies:
         copy.start()
 
@@ -171,7 +176,13 @@
         [
             jnp.sum(emb * emb, axis=0, keepdims=True),
             jnp.sum(hid * hid, axis=0, keepdims=True),
-            rows_ref[0:4],
+            jnp.concatenate(
+                [
+                    jnp.concatenate([g[...].astype(f32) for g in gains], axis=0),
+                    jnp.zeros((4, ROWS - FEAT), f32),
+                ],
+                axis=1,
+            ),
             jnp.zeros((2, ROWS), f32),
         ],
         axis=0,
@@ -438,19 +449,6 @@
     waits.send([q_copy(k, z) for k in (1, 3, 2)])
     for k in (1, 3, 2):
         waits.expect("q%d" % k, q_copy(k, (z + 4 - k) % 4).wait_recv)
-    ha.wait("Lc", "Pc")
-    hb.wait("Lc", "Pc")
-    hc.wait("Sc")
-
-    def norm(xr, _):
-        gain = small[xr].reshape(16, 8, ROWS)[:, 3, :128].T
-        for yr in range(4):
-            for zr in range(4):
-                block = gath[xr, yr, zr].astype(f32) * hid_scale * gain[:FEAT, yr * 4 + zr : yr * 4 + zr + 1]
-                normed[(x + xr) % 4, (y + yr) % 4, (z + zr) % 4] = block.astype(bf16)
-        return 0
-
-    lax.fori_loop(0, 4, norm, 0)
     for copy in head_copies:
         copy.wait()
     for k in (1, 3, 2):
@@ -476,10 +474,23 @@
         g.start("Lb")
     for g in gs:
         g.start("Lc")
-    main_dot(0)
     for g in gs:
         g.wait("Lb")
         g.start("Pc")
+    ha.wait("Lc", "Pc")
+    hb.wait("Lc", "Pc")
+    hc.wait("Sc")
+
+    def norm(xr, _):
+        gain = small[xr].reshape(16, 8, ROWS)[:, 3, :128].T
+        for yr in range(4):
+            for zr in range(4):
+                block = gath[xr, yr, zr].astype(f32) * hid_scale * gain[:FEAT, yr * 4 + zr : yr * 4 + zr + 1]
+                normed[(x + xr) % 4, (y + yr) % 4, (z + zr) % 4] = block.astype(bf16)
+        return 0
+
+    lax.fori_loop(0, 4, norm, 0)
+    main_dot(0)
     main_dot(1)
     main_dot(2)
     main_dot(3)
@@ -537,19 +548,24 @@
         copy.wait_send()
     waits.sends = waits.sends[len(earlier) :]
 
-    for g in gs:
-        g.wait("Lc", "Pc")
-
-    def draft_dot(zr):
-        there = pl.ds(pl.multiple_of(((z + zr) % 4) * QUART, 128), QUART)
-        rows = jnp.dot(gd[:, :, zr].reshape(ROWS, QUART), head[there], preferred_element_type=f32)
-        acc[...] = rows if zr == 0 else acc[...] + rows
-
-    draft_dot(0)
-    draft_dot(1)
+    def draft_dot(p):
+        c, n = G_PARTS[p]
+        rows = None
+        for zr in range(4):
+            there = pl.ds(pl.multiple_of((z + zr) % 4 * QUART + c, 128), n)
+            term = jnp.dot(
+                gd[:, :, zr, :, c : c + n].reshape(ROWS, n), head[there], preferred_element_type=f32
+            )
+            rows = term if rows is None else rows + term
+        return rows
+
+    gs[2].wait("Lc", "Pc")
+    acc[...] = draft_dot(2)
     st_start(0, 1, st_finish(0, 0))
-    draft_dot(2)
-    draft_dot(3)
+    gs[0].wait("Lc", "Pc")
+    acc[...] += draft_dot(0)
+    gs[1].wait("Lc", "Pc")
+    acc[...] += draft_dot(1)
     for xr in range(4):
         for yr in range(4):
             to = ((x + xr) % 4) * 4 + (y + yr) % 4
@@ -603,8 +619,6 @@
     token_ids,
     row_request,
 ):
-    rows = jnp.stack([draft_gain, final_gain, hidden_gain, embed_gain]).astype(f32)
-    rows = jnp.pad(rows, ((0, 4), (0, ROWS - FEAT)))
     vmem = pl.BlockSpec(memory_space=pltpu.VMEM)
     hbm = pl.BlockSpec(memory_space=pltpu.HBM)
     main, draft, main_lse, draft_lse, score = pl.pallas_call(
@@ -617,11 +631,15 @@
             jax.ShapeDtypeStruct((1, ROWS), f32),
             jax.ShapeDtypeStruct((1, REQS), f32),
         ),
-        in_specs=[hbm] * 2 + [vmem] + [hbm] * 5,
+        in_specs=[hbm] * 11,
         out_specs=(hbm,) * 2 + (vmem,) * 3,
         scratch_shapes=[
             pltpu.VMEM((ROWS, VOC), f32),
             pltpu.VMEM((ROWS, VOC), f32),
+            pltpu.VMEM((1, FEAT), bf16),
+            pltpu.VMEM((1, FEAT), bf16),
+            pltpu.VMEM((1, FEAT), bf16),
+            pltpu.VMEM((1, FEAT), bf16),
             pltpu.VMEM((1, ROWS), jnp.int32),
             pltpu.VMEM((1, ROWS), jnp.int32),
             pltpu.VMEM((D, VOC), bf16),
@@ -644,7 +662,7 @@
             pltpu.VMEM((2, 3, 4, 8, ROWS), f32),
             pltpu.VMEM((2, REQS, 128), f32),
             DMA((4,)),
-            DMA((9,)),
+            DMA((13,)),
             DMA((9,)),
             DMA((9,)),
             DMA((2, 6)),
@@ -673,7 +691,10 @@
     )(
         hidden.T,
         next_embedding.T,
-        rows,
+        draft_gain[None, :],
+        final_gain[None, :],
+        hidden_gain[None, :],
+        embed_gain[None, :],
         token_ids[None, :],
         row_request[None, :],
         head_weight,

time: 104 us -> 100 us (0.962)
  Pallas kernels: 97.8 us -> 96.1 us
  other arithmetic: 4.38 us -> 3.07 us
    pallas_call x1, Pallas kernels: 97.8 us -> 96.1 us  [per_device(): pl.pallas_call(kernel, name='heads', out_shape=(jax.ShapeDtypeStruct((ROW...]
    pad x1 -> x0, other arithmetic: 1.31 us -> none  [per_device(): rows = jnp.pad(rows, ((0, 4), (0, ROWS - FEAT)))]
where the time goes in v4:
time: 100 us
  Pallas kernels  96.1 us (96%)
  other arithmetic  3.07 us (3%)
    pallas_call x1, Pallas kernels, per_device(): pl.pallas_call(kernel, name='heads', out_shape=(jax.ShapeDtypeStruct((ROW...  96.1 us
    sub x1, other arithmetic, per_device(): draft - draft_lse[0][:, None]  3.07 us

profile of v4, /device:TPU:0, one launch (start us, length us, event | category | flops | bytes accessed | tf_op | source)
XLA Modules:
  0.0 100.3 jit_solution(8499070355774274938)
XLA Ops:
  0.6 96.1 %heads.1 = (f32[256,1024]{1,0:T(8,128)}, f32[256,1024]{1,0:T(8,128)}, f32[1,256]{1,0:T(1,128)}, f32[1,256]{1,0:T(1,128)}, f32[1,64]{1,0:T(1,128)}) custom-call(bf16[112,256]{1,0:T(8,128)(2,1)} %bitcast.13, bf16[112,256]{1,0:T(8,128)(2,1)} %bitcast.14, bf16[1,112]{1,0:T(2,128)(2,1)} %bitcast.17, bf16[1,112]{1,0:T(2,128)(2,1)} %bitcast.18, ...), custom_call_target="tpu_custom_call" | custom-call | flops 8300000256 | bytes 20000000 | tf_op jit(solution)/shard_map/heads/pallas_call | solution.py:624
  96.7 0.0 copy-start
  96.8 3.1 %broadcast_subtract_fusion = (f32[256,1024]{1,0:T(8,128)}, f32[256,1024]{1,0:T(8,128)}) fusion(f32[256,1024]{1,0:T(8,128)} %get-tuple-element.10, f32[256]{0:T(256)} %bitcast.12, f32[256,1024]{1,0:T(8,128)} %get-tuple-element.8, f32[256]{0:T(256)} %bitcast.11), kind=kLoop, calls=%fused_computation | loop fusion | flops 524288 | bytes 4196352 | tf_op jit(solution)/shard_map/sub | solution.py:704
  99.8 0.0 copy-done
  99.8 0.5 copy.15
Async XLA Ops:
  96.7 3.1 %copy-start = (f32[1,64]{1,0:T(1,128)S(1)}, f32[1,64]{1,0:T(1,128)}, u32[]{:S(2)}) copy-start(f32[1,64]{1,0:T(1,128)} %get-tuple-element.12) | copy-start | bytes 772
